TPU v7x, 32 devices: a whole 2x2x4 slice. The times are simulated.
32 devices in a mesh: row: 4 (over z), col: 8 (over y, x, core).
Axes of the slice: x: 2, y: 2, z: 4, core: 2. Of those that a mesh axis runs over, the one named last changes fastest.
Arguments:
- source_tiles: bfloat16 [4, 8, 1024, 128], P('row', 'col'), may hold values from -6 to 6
- requests: int32 [4, 8, 8, 256], P('row', 'col'), may hold values from 0 to 1023
- stencil: int32 [128, 256, 4], P('row', 'col'), may hold values from 0 to 2047, as said below
- regrid_weight: float32 [128, 256, 4], P('row', 'col'), may hold values from 0.1 to 0.6
- w_in: bfloat16 [3, 3, 64, 128], replicated, may hold values from -0.4375 to 0.4375
- w_enc: bfloat16 [3, 3, 128, 128], replicated, may hold values from -0.3125 to 0.3125
- w_mid_first: bfloat16 [3, 3, 128, 128], replicated, may hold values from -0.3125 to 0.3125
- w_mid_second: bfloat16 [3, 3, 128, 128], replicated, may hold values from -0.3125 to 0.3125
- w_dec_first: bfloat16 [3, 3, 256, 128], replicated, may hold values from -0.21875 to 0.21875
- w_dec_second: bfloat16 [3, 3, 128, 128], replicated, may hold values from -0.3125 to 0.3125
- w_out: bfloat16 [128, 64], replicated, may hold values from -0.75 to 0.75
Outputs:
- forecast: bfloat16 [128, 256, 2, 64], P('row', 'col')
Inputs may be any that keep to these rules, and one draw needn't show every extreme that they name: `stencil`: within each device's 32 x 32 block of target cells, every slot 0 to 2047 appears at least once among the entries.
All inputs are finite; a program needn't handle non-finite values.
Results may differ from a plain program's by a relative error of at most 0.017.
Values may be sent and summed in bfloat16 or wider, within the bound.
A program may use at most 64 MiB of HBM per device.

v0:
```python
import functools

import jax
import jax.numpy as jnp
from jax import lax
from jax.experimental import pallas as pl
from jax.experimental.pallas import tpu as pltpu
from jax.sharding import PartitionSpec as P

FIELDS = 64
CH = 128
HALO = 8


def silu(a):
    return a * (0.5 + 0.5 * jnp.tanh(0.5 * a))


def unet_kernel(
    tile_rows, tile_cols, p_ref, w_in, w_enc, w_m1, w_m2, w_d1, w_d2, w_out, out_ref,
    first, skip, pooled, middle, up, dec1, tmp, c_in, c_enc, c_m1, c_m2, c_d1, c_d2, c_out, pairs,
):
    wide = tile_cols + 2 * HALO
    half = wide // 2
    row = lax.axis_index("row")
    at_top = row == 0
    at_bottom = row == lax.axis_size("row") - 1
    f32, bf16 = jnp.float32, jnp.bfloat16

    c_in[...] = jnp.zeros_like(c_in)
    c_out[...] = jnp.zeros_like(c_out)
    w_last = w_out[...].astype(f32).T.astype(bf16)
    for b in range(2):
        c_out[b * CH : (b + 1) * CH, b * FIELDS : (b + 1) * FIELDS] = w_last
    size = p_ref.shape[0]
    values = p_ref[...].astype(f32)
    turned = pltpu.roll(values, FIELDS, 1)
    below = pltpu.roll(values, size - wide, 0)
    turned_below = pltpu.roll(turned, size - wide, 0)
    low = lax.broadcasted_iota(jnp.int32, (size, CH), 1) < FIELDS
    pairs[0] = jnp.where(low, values, turned_below).astype(bf16)
    pairs[1] = jnp.where(low, turned, below).astype(bf16)
    for dy in range(3):
        for dx in range(3):
            rows = slice(dy * CH, (dy + 1) * CH)
            cols = slice(dx * CH, (dx + 1) * CH)
            c_in[dy * FIELDS : (dy + 1) * FIELDS, cols] = w_in[dy, dx]
            c_enc[rows, cols] = w_enc[dy, dx]
            c_m1[rows, cols] = w_m1[dy, dx]
            c_m2[rows, cols] = w_m2[dy, dx]
            c_d1[rows, cols] = w_d1[dy, dx, :CH]
            c_d1[(dy + 3) * CH : (dy + 4) * CH, cols] = w_d1[dy, dx, CH:]
            c_d2[rows, cols] = w_d2[dy, dx]

    def conv(sources, weight, width, chunk_rows, start, steps=(0, 1, 2)):
        size = chunk_rows * width
        windows = [
            load(pl.multiple_of(start + (offset + dy) * width, 8), size).astype(bf16)
            for load, offset in sources
            for dy in steps
        ]
        u = jnp.dot(jnp.concatenate(windows, axis=1), weight[...], preferred_element_type=f32)
        return silu(
            u[:, CH : 2 * CH]
            + pltpu.roll(u[:, :CH], 1, 0)
            + pltpu.roll(u[:, 2 * CH :], size - 1, 0)
        )

    def per_chunk(height, chunk_rows, width, step):
        chunks = height // chunk_rows

        @pl.loop(0, 2 * chunks)
        def _(i):
            b = i // chunks
            start = pl.multiple_of((i % chunks) * (chunk_rows * width), 8)
            step(b, start)

    def clear(ref, depth, inner, width):
        @pl.when(at_top)
        def _():
            ref[:, : depth * width] = jnp.zeros((2, depth * width, CH), ref.dtype)

        @pl.when(at_bottom)
        def _():
            ref[:, (depth + inner) * width :] = jnp.zeros((2, depth * width, CH), ref.dtype)

    def reader(ref, b):
        return lambda start, size: ref[b, pl.ds(start, size), :]

    h_first = tile_rows + 14
    h_skip = tile_rows + 12
    h_pool = h_skip // 2
    h_mid = h_pool - 2
    h_coarse = h_mid - 2
    h_dec1 = tile_rows + 2

    def first_step(b, start):
        chunk = h_first // 2
        value = conv([(reader(pairs, b), 0)], c_in, wide, chunk, start, (0, 2))
        first[b, pl.ds(start, chunk * wide), :] = value.astype(bf16)

    per_chunk(h_first, h_first // 2, wide, first_step)
    clear(first, 7, tile_rows, wide)

    def skip_step(b, start):
        chunk = h_skip // 2
        value = conv([(reader(first, b), 0)], c_enc, wide, chunk, start)
        skip[b, pl.ds(start, chunk * wide), :] = value.astype(bf16)

    per_chunk(h_skip, h_skip // 2, wide, skip_step)
    clear(skip, 6, tile_rows, wide)

    @pl.loop(0, 2)
    def _(b):
        s = skip[b].astype(f32).reshape(h_pool, 2 * wide, CH)
        tmp[: h_pool * wide, :] = (s[:, :wide] + s[:, wide:]).reshape(h_pool * wide, CH)
        total = (
            tmp[pl.ds(0, h_pool * half, stride=2), :] + tmp[pl.ds(1, h_pool * half, stride=2), :]
        )
        pooled[b] = (total * 0.25).astype(bf16).astype(f32)

    def mid_step(b, start):
        value = conv([(reader(pooled, b), 0)], c_m1, half, h_mid, start)
        middle[b, pl.ds(start, h_mid * half), :] = value.astype(bf16).astype(f32)

    per_chunk(h_mid, h_mid, half, mid_step)
    clear(middle, 2, tile_rows // 2, half)

    @pl.loop(0, 2)
    def _(b):
        value = conv([(reader(middle, b), 0)], c_m2, half, h_coarse, 0)
        size = h_coarse * half
        tmp[pl.ds(0, size, stride=2), :] = value
        tmp[pl.ds(1, size, stride=2), :] = value
        v = tmp[: h_coarse * wide, :].astype(bf16).reshape(h_coarse, 1, wide, CH)
        up[b] = jnp.broadcast_to(v, (h_coarse, 2, wide, CH)).reshape(2 * h_coarse * wide, CH)

    clear(up, 2, tile_rows, wide)

    def dec1_step(b, start):
        chunk = h_dec1 // 2
        value = conv([(reader(up, b), 0), (reader(skip, b), 4)], c_d1, wide, chunk, start)
        dec1[b, pl.ds(start, chunk * wide), :] = value.astype(bf16)

    per_chunk(h_dec1, h_dec1 // 2, wide, dec1_step)
    clear(dec1, 1, tile_rows, wide)

    chunk = tile_rows // 2

    @pl.loop(0, 2)
    def _(i):
        start = pl.multiple_of(i * (chunk * wide), 8)
        both = []
        for b in range(2):
            value = conv([(reader(dec1, b), 0)], c_d2, wide, chunk, start)
            value = value.reshape(chunk, wide, CH)[:, HALO : HALO + tile_cols]
            both.append(value.reshape(chunk * tile_cols, CH).astype(bf16))
        result = jnp.dot(
            jnp.concatenate(both, axis=1), c_out[...], preferred_element_type=f32
        )
        place = pl.multiple_of(i * (chunk * tile_cols), 8)
        out_ref[pl.ds(place, chunk * tile_cols), :] = result.astype(bf16)


def unet(padded, tile_rows, tile_cols, weights):
    wide = tile_cols + 2 * HALO
    half = wide // 2
    f32, bf16 = jnp.float32, jnp.bfloat16
    square = pltpu.VMEM((3 * CH, 3 * CH), bf16)
    scratch = [
        pltpu.VMEM((2, (tile_rows + 14) * wide, CH), bf16),
        pltpu.VMEM((2, (tile_rows + 12) * wide, CH), bf16),
        pltpu.VMEM((2, (tile_rows // 2 + 6) * half, CH), f32),
        pltpu.VMEM((2, (tile_rows // 2 + 4) * half, CH), f32),
        pltpu.VMEM((2, (tile_rows + 4) * wide, CH), bf16),
        pltpu.VMEM((2, (tile_rows + 2) * wide, CH), bf16),
        pltpu.VMEM(((tile_rows // 2 + 6) * wide, CH), f32),
        pltpu.VMEM((4 * FIELDS, 3 * CH), bf16),
        square, square, square,
        pltpu.VMEM((6 * CH, 3 * CH), bf16),
        square,
        pltpu.VMEM((2 * CH, 2 * FIELDS), bf16),
        pltpu.VMEM((2, (tile_rows + 2 * HALO) * wide, CH), bf16),
    ]
    return pl.pallas_call(
        functools.partial(unet_kernel, tile_rows, tile_cols),
        out_shape=jax.ShapeDtypeStruct((tile_rows * tile_cols, 2 * FIELDS), bf16),
        in_specs=[pl.BlockSpec(memory_space=pltpu.VMEM)] * 8,
        out_specs=pl.BlockSpec(memory_space=pltpu.VMEM),
        scratch_shapes=scratch,
        compiler_params=pltpu.CompilerParams(vmem_limit_bytes=44 * 1024 * 1024),
        cost_estimate=pl.CostEstimate(
            flops=6 * 10**9, bytes_accessed=4 * 10**6, transcendentals=2 * 10**6
        ),
    )(padded, *weights[:-1], weights[-1].T)


MESH = pl.DeviceIdType.MESH


def regrid_kernel(
    tile_rows, tile_cols, src_in, req_in, sten_in, wgt_in, out_ref,
    src_ref, req_ref, sten_ref, wgt_ref, load, reqs, src_t, mix, outbox, inbox, acc, pad, slot_rows, weight_rows,
    req_send, req_recv, box_send, box_recv, halo_send, halo_recv,
):
    f32, bf16 = jnp.float32, jnp.bfloat16
    row, me = lax.axis_index("row"), lax.axis_index("col")
    n_row, n = lax.axis_size("row"), lax.axis_size("col")
    cap = req_ref.shape[1]
    cells = src_ref.shape[0]
    spots = tile_rows * tile_cols
    has_up, has_down = row > 0, row < n_row - 1
    blocks = tile_cols // HALO
    edge = HALO * HALO
    inner = tile_rows * HALO

    loads = [
        pltpu.make_async_copy(outer, held, load.at[i])
        for i, (outer, held) in enumerate(
            [(req_in, req_ref), (src_in, src_ref), (sten_in, sten_ref), (wgt_in, wgt_ref)]
        )
    ]
    for copy in loads:
        copy.start()

    barrier = pltpu.get_barrier_semaphore()

    def greet(r, c):
        pl.semaphore_signal(
            barrier, inc=1, device_id=(r, lax.rem(c + n, n)), device_id_type=MESH
        )

    @pl.loop(1, n)
    def _(step):
        greet(row, me + step)

    @pl.when(has_up)
    def _():
        for d in (-1, 0, 1):
            greet(row - 1, me + d)

    @pl.when(has_down)
    def _():
        for d in (-1, 0, 1):
            greet(row + 1, me + d)

    rows_beside = jnp.minimum(row, 1) + jnp.minimum(n_row - 1 - row, 1)
    pl.semaphore_wait(barrier, n - 1 + 3 * rows_beside)

    loads[0].wait()

    def ask(step, sender):
        return pltpu.make_async_remote_copy(
            src_ref=req_ref,
            dst_ref=reqs.at[sender],
            send_sem=req_send.at[step],
            recv_sem=req_recv.at[sender],
            device_id=(row, lax.rem(me + step, n)),
            device_id_type=MESH,
        )

    @pl.loop(1, n)
    def _(step):
        ask(step, me).start()

    reqs[me] = req_ref[...]
    loads[1].wait()
    src_t[...] = src_ref[...].astype(f32).T.astype(bf16)

    loads[2].wait()
    loads[3].wait()
    taps = sten_ref.shape[1]
    for k in range(taps):
        slot_rows[k : k + 1, :] = jnp.concatenate(
            [sten_ref[y, k : k + 1, :] for y in range(tile_rows)], axis=1
        ).astype(f32)
        weight_rows[k : k + 1, :] = jnp.concatenate(
            [wgt_ref[y, k : k + 1, :] for y in range(tile_rows)], axis=1
        )
    tile, piece = 16, 256

    def ladder(width):
        return lax.broadcasted_iota(jnp.int32, (tile, width), 0).astype(f32).astype(bf16)

    def spread(values):
        return jnp.broadcast_to(values, (tile, values.shape[1])).astype(bf16)

    lanes = min(512, spots)
    zero, one = jnp.zeros((), bf16), jnp.ones((), bf16)

    def mix_block(j):
        for left_lane in range(0, spots, lanes):
            here = slice(left_lane, left_lane + lanes)
            ids = ladder(lanes)
            weights = [spread(weight_rows[k : k + 1, here]) for k in range(taps)]
            for start in range(0, cap, piece):
                base = (j * cap + start).astype(f32)
                near = [spread(slot_rows[k : k + 1, here] - base) for k in range(taps)]
                for g in range(0, min(piece, cap), tile):
                    step_ids = ids + jnp.asarray(g, bf16)
                    total = None
                    for k in range(taps):
                        part = jnp.where(step_ids == near[k], weights[k], zero)
                        total = part if total is None else total + part
                    mix[j, start + g : start + g + tile, here] = total

    @pl.loop(0, n // 2)
    def _(j):
        mix_block(j)

    def picked(dest):
        asked = reqs[dest, pl.ds(me, 1), :].astype(f32)
        ids = ladder(cap)
        rows = []
        for start in range(0, cells, piece):
            near = spread(asked - float(start))
            for g in range(0, piece, tile):
                rows.append(jnp.where(ids + jnp.asarray(g, bf16) == near, one, zero))
        hot = jnp.concatenate(rows, axis=0)
        return jnp.dot(src_t[...], hot, preferred_element_type=f32).astype(bf16)

    def post(step, sender):
        return pltpu.make_async_remote_copy(
            src_ref=outbox.at[step],
            dst_ref=inbox.at[sender],
            send_sem=box_send.at[step],
            recv_sem=box_recv.at[sender],
            device_id=(row, lax.rem(me + step, n)),
            device_id_type=MESH,
        )

    @pl.loop(1, n)
    def _(step):
        dest = lax.rem(me + step, n)
        ask(step, dest).wait_recv()
        outbox[step] = picked(dest)
        post(step, me).start()

    inbox[me] = picked(me)

    @pl.loop(n // 2, n)
    def _(j):
        mix_block(j)

    acc[...] = jnp.dot(inbox[me], mix[me], preferred_element_type=f32)

    @pl.loop(1, n)
    def _(step):
        sender = lax.rem(me - step + n, n)
        post(step, sender).wait_recv()
        acc[...] += jnp.dot(inbox[sender], mix[sender], preferred_element_type=f32)

    grid = acc[...].T.reshape(tile_rows, blocks, HALO, 2 * FIELDS)
    for xb in range(blocks):
        pad[xb + 1, edge : edge + inner, :] = (
            grid[:, xb].reshape(inner, 2 * FIELDS).astype(bf16)
        )

    @pl.when(jnp.logical_not(has_up))
    def _():
        pad[:, :edge] = jnp.zeros((blocks + 2, edge, 2 * FIELDS), bf16)

    @pl.when(jnp.logical_not(has_down))
    def _():
        pad[:, edge + inner :] = jnp.zeros((blocks + 2, edge, 2 * FIELDS), bf16)

    mid = slice(edge, edge + inner)
    first, last = slice(edge, 2 * edge), slice(inner, inner + edge)
    low, high = slice(0, edge), slice(edge + inner, 2 * edge + inner)
    every = slice(1, blocks + 1)
    left, right = slice(1, 2), slice(blocks, blocks + 1)
    before, after = slice(0, 1), slice(blocks + 1, blocks + 2)
    moves = [
        (0, 1, (right, mid), (before, mid)),
        (0, -1, (left, mid), (after, mid)),
        (1, 0, (every, last), (every, low)),
        (1, 1, (right, last), (before, low)),
        (1, -1, (left, last), (after, low)),
        (-1, 0, (every, first), (every, high)),
        (-1, 1, (right, first), (before, high)),
        (-1, -1, (left, first), (after, high)),
    ]

    def shift(i):
        dr, dc, src, dst = moves[i]
        return pltpu.make_async_remote_copy(
            src_ref=pad.at[src[0], src[1]],
            dst_ref=pad.at[dst[0], dst[1]],
            send_sem=halo_send.at[i],
            recv_sem=halo_recv.at[i],
            device_id=(row + dr, lax.rem(me + dc + n, n)),
            device_id_type=MESH,
        )

    @pl.when(has_down)
    def _():
        for i in (2, 3, 4):
            shift(i).start()

    @pl.when(has_up)
    def _():
        for i in (5, 6, 7):
            shift(i).start()

    for i in (0, 1):
        shift(i).start()
    for i in (0, 1):
        shift(i).wait()

    @pl.when(has_up)
    def _():
        for i in (2, 3, 4):
            shift(i).wait_recv()

    @pl.when(has_down)
    def _():
        for i in (5, 6, 7):
            shift(i).wait_recv()

    parts = [
        pad[xb].astype(f32).reshape(tile_rows + 2 * HALO, HALO, 2 * FIELDS)
        for xb in range(blocks + 2)
    ]
    out_ref[...] = jnp.concatenate(parts, axis=1).reshape(out_ref.shape).astype(bf16)

    @pl.when(has_down)
    def _():
        for i in (2, 3, 4):
            shift(i).wait_send()

    @pl.when(has_up)
    def _():
        for i in (5, 6, 7):
            shift(i).wait_send()

    @pl.loop(1, n)
    def _(step):
        ask(step, me).wait_send()
        post(step, me).wait_send()


def regrid(source, wanted, stencil, weight, tile_rows, tile_cols):
    f32, bf16 = jnp.float32, jnp.bfloat16
    n, cap = wanted.shape
    cells, columns = source.shape
    spots = tile_rows * tile_cols
    blocks = tile_cols // HALO
    rows = tile_rows + 2 * HALO
    dma = pltpu.SemaphoreType.DMA
    return pl.pallas_call(
        functools.partial(regrid_kernel, tile_rows, tile_cols),
        out_shape=jax.ShapeDtypeStruct((rows * (tile_cols + 2 * HALO), columns), bf16),
        in_specs=[pl.BlockSpec(memory_space=pltpu.HBM)] * 4,
        out_specs=pl.BlockSpec(memory_space=pltpu.VMEM),
        scratch_shapes=[
            pltpu.VMEM(source.shape, bf16),
            pltpu.VMEM(wanted.shape, jnp.int32),
            pltpu.VMEM(stencil.shape, jnp.int32),
            pltpu.VMEM(weight.shape, f32),
            dma((4,)),
            pltpu.VMEM((n, n, cap), jnp.int32),
            pltpu.VMEM((columns, cells), bf16),
            pltpu.VMEM((n, cap, spots), bf16),
            pltpu.VMEM((n, columns, cap), bf16),
            pltpu.VMEM((n, columns, cap), bf16),
            pltpu.VMEM((columns, spots), f32),
            pltpu.VMEM((blocks + 2, rows * HALO, columns), bf16),
            pltpu.VMEM((stencil.shape[1], spots), f32),
            pltpu.VMEM((stencil.shape[1], spots), f32),
            dma((n,)), dma((n,)), dma((n,)), dma((n,)), dma((8,)), dma((8,)),
        ],
        compiler_params=pltpu.CompilerParams(
            collective_id=0, has_side_effects=True, vmem_limit_bytes=56 * 1024 * 1024
        ),
        cost_estimate=pl.CostEstimate(
            flops=10**9, bytes_accessed=2 * 10**6, transcendentals=0
        ),
    )(source, wanted, stencil, weight)


def body(source_tiles, requests, stencil, regrid_weight, *weights):
    tile_rows, tile_cols = stencil.shape[:2]
    cells, columns = source_tiles.shape[2:]
    padded = regrid(
        source_tiles.reshape(cells, columns),
        requests.reshape(requests.shape[2:]),
        stencil.transpose(0, 2, 1),
        regrid_weight.transpose(0, 2, 1),
        tile_rows,
        tile_cols,
    )
    result = unet(padded, tile_rows, tile_cols, weights)
    return result.reshape(tile_rows, tile_cols, 2, FIELDS)


def solution(mesh):
    placed = (P("row", "col", None, None),) * 2 + (P("row", "col", None),) * 2 + (P(),) * 7
    return jax.shard_map(
        body, mesh=mesh, in_specs=placed, out_specs=P("row", "col", None, None), check_vma=False
    )
```

profile of v0, /device:TPU:0, one launch (start us, length us, event | category | flops | bytes accessed | tf_op | source)
XLA Modules:
  0.0 37.4 jit_solution(715196174473153236)
XLA Ops:
  0.0 0.0 copy-start
  0.0 0.0 copy-start.1
  0.0 0.0 copy-start.2
  0.0 0.0 copy-start.3
  0.0 0.0 copy-start.4
  0.0 0.0 copy-start.5
  0.0 0.0 copy-start.6
  0.0 22.2 %shard_map.109.p_ref = bf16[2304,128]{1,0:T(8,128)(2,1)} custom-call(bf16[1024,128]{1,0:T(8,128)(2,1)} %bitcast.6, s32[8,256]{1,0:T(8,128)} %bitcast.9, s32[32,4,32]{2,1,0:T(4,128)} %bitcast.7, f32[32,4,32]{2,1,0:T(4,128)} %bitcast.8), custom_call_target="tpu_custom_call" | custom-call | flops 1000000000 | bytes 2000000 | tf_op jit(solution)/shard_map/pallas_call | solution.py:450
  22.2 0.0 copy-done
  22.2 0.0 copy-done.1
  22.2 0.0 copy-done.2
  22.3 0.0 copy-done.3
  22.3 0.0 copy-done.4
  22.3 0.0 copy-done.5
  22.3 0.0 copy-done.6
  22.3 0.0 copy-start.7
  22.3 1.1 %copy-done.7 = bf16[2304,128]{1,0:T(8,128)(2,1)S(1)} copy-done((bf16[2304,128]{1,0:T(8,128)(2,1)S(1)}, bf16[2304,128]{1,0:T(8,128)(2,1)}, u32[]{:S(2)}) %copy-start.7) | copy-done | bytes 589848
  23.4 13.0 %shard_map.110 = bf16[1024,128]{1,0:T(8,128)(2,1)S(1)} custom-call(bf16[2304,128]{1,0:T(8,128)(2,1)S(1)} %copy-done.7, bf16[3,3,64,128]{3,2,1,0:T(8,128)(2,1)S(1)} %copy-done.5, bf16[3,3,128,128]{3,2,1,0:T(8,128)(2,1)S(1)} %copy-done.1, bf16[3,3,128,128]{3,2,1,0:T(8,128)(2,1)S(1)} %copy-done.2, bf16[3,3,128,128]{3,2,1,0:T(8,128)(2,1)S(1)} %copy-done.3, ...), custom_call_target="tpu_custom_call" | custom-call | flops 6000000000 | bytes 4000000 | tf_op jit(solution)/shard_map/pallas_call | solution.py:185
  36.3 1.1 %reshape.11 = bf16[32,32,2,64]{3,2,1,0:T(2,128)(2,1)} reshape(bf16[1024,128]{1,0:T(8,128)(2,1)S(1)} %shard_map.110) | data formatting | bytes 524288 | tf_op jit(solution)/shard_map/reshape | solution.py:493
Async XLA Ops:
  0.0 22.2 %copy-start = (bf16[3,3,256,128]{3,2,1,0:T(8,128)(2,1)S(1)}, bf16[3,3,256,128]{3,2,1,0:T(8,128)(2,1)}, u32[]{:S(2)}) copy-start(bf16[3,3,256,128]{3,2,1,0:T(8,128)(2,1)} %w_d1.1) | copy-start | bytes 1769476
  0.0 22.2 %copy-start.1 = (bf16[3,3,128,128]{3,2,1,0:T(8,128)(2,1)S(1)}, bf16[3,3,128,128]{3,2,1,0:T(8,128)(2,1)}, u32[]{:S(2)}) copy-start(bf16[3,3,128,128]{3,2,1,0:T(8,128)(2,1)} %w_enc.1) | copy-start | bytes 884740
  0.0 22.2 %copy-start.2 = (bf16[3,3,128,128]{3,2,1,0:T(8,128)(2,1)S(1)}, bf16[3,3,128,128]{3,2,1,0:T(8,128)(2,1)}, u32[]{:S(2)}) copy-start(bf16[3,3,128,128]{3,2,1,0:T(8,128)(2,1)} %w_m1.1) | copy-start | bytes 884740
  0.0 22.3 %copy-start.3 = (bf16[3,3,128,128]{3,2,1,0:T(8,128)(2,1)S(1)}, bf16[3,3,128,128]{3,2,1,0:T(8,128)(2,1)}, u32[]{:S(2)}) copy-start(bf16[3,3,128,128]{3,2,1,0:T(8,128)(2,1)} %w_m2.1) | copy-start | bytes 884740
  0.0 22.3 %copy-start.4 = (bf16[3,3,128,128]{3,2,1,0:T(8,128)(2,1)S(1)}, bf16[3,3,128,128]{3,2,1,0:T(8,128)(2,1)}, u32[]{:S(2)}) copy-start(bf16[3,3,128,128]{3,2,1,0:T(8,128)(2,1)} %w_d2.1) | copy-start | bytes 884740
  0.0 22.3 %copy-start.5 = (bf16[3,3,64,128]{3,2,1,0:T(8,128)(2,1)S(1)}, bf16[3,3,64,128]{3,2,1,0:T(8,128)(2,1)}, u32[]{:S(2)}) copy-start(bf16[3,3,64,128]{3,2,1,0:T(8,128)(2,1)} %w_in.1) | copy-start | bytes 442372
  0.0 22.3 %copy-start.6 = (bf16[128,64]{0,1:T(8,128)(2,1)S(1)}, bf16[128,64]{0,1:T(8,128)(2,1)}, u32[]{:S(2)}) copy-start(bf16[128,64]{0,1:T(8,128)(2,1)} %param.21) | copy-start | bytes 49156
  22.3 1.1 %copy-start.7 = (bf16[2304,128]{1,0:T(8,128)(2,1)S(1)}, bf16[2304,128]{1,0:T(8,128)(2,1)}, u32[]{:S(2)}) copy-start(bf16[2304,128]{1,0:T(8,128)(2,1)} %shard_map.109.p_ref) | copy-start | bytes 1769476
where the time goes:
time: 37.5 us; the launch traced here: 37.4 us
  Pallas kernels  35.1 us (94%)
  local copies, waits for them, and re-layouts  2.14 us (6%)
    pallas_call x1, Pallas kernels, regrid(): pl.pallas_call(functools.partial(regrid_kernel, tile_rows, tile_cols), ou...  22.2 us
    pallas_call x1, Pallas kernels, unet(): pl.pallas_call(functools.partial(unet_kernel, tile_rows, tile_cols), out_...  13 us
    unnamed x16, local copies, waits for them, and re-layouts  1.08 us
    reshape x1, local copies, waits for them, and re-layouts, body(): return result.reshape(tile_rows, tile_cols, 2, FIELDS)  1.06 us

commit v1 on v0

--- a/solution.py
+++ b/solution.py
@@ -162,12 +162,12 @@
         out_ref[pl.ds(place, chunk * tile_cols), :] = result.astype(bf16)
 
 
-def unet(padded, tile_rows, tile_cols, weights):
+def unet_scratch(tile_rows, tile_cols):
     wide = tile_cols + 2 * HALO
     half = wide // 2
     f32, bf16 = jnp.float32, jnp.bfloat16
     square = pltpu.VMEM((3 * CH, 3 * CH), bf16)
-    scratch = [
+    return [
         pltpu.VMEM((2, (tile_rows + 14) * wide, CH), bf16),
         pltpu.VMEM((2, (tile_rows + 12) * wide, CH), bf16),
         pltpu.VMEM((2, (tile_rows // 2 + 6) * half, CH), f32),
@@ -182,24 +182,25 @@
         pltpu.VMEM((2 * CH, 2 * FIELDS), bf16),
         pltpu.VMEM((2, (tile_rows + 2 * HALO) * wide, CH), bf16),
     ]
-    return pl.pallas_call(
-        functools.partial(unet_kernel, tile_rows, tile_cols),
-        out_shape=jax.ShapeDtypeStruct((tile_rows * tile_cols, 2 * FIELDS), bf16),
-        in_specs=[pl.BlockSpec(memory_space=pltpu.VMEM)] * 8,
-        out_specs=pl.BlockSpec(memory_space=pltpu.VMEM),
-        scratch_shapes=scratch,
-        compiler_params=pltpu.CompilerParams(vmem_limit_bytes=44 * 1024 * 1024),
-        cost_estimate=pl.CostEstimate(
-            flops=6 * 10**9, bytes_accessed=4 * 10**6, transcendentals=2 * 10**6
-        ),
-    )(padded, *weights[:-1], weights[-1].T)
 
 
 MESH = pl.DeviceIdType.MESH
 
 
+def whole_kernel(tile_rows, tile_cols, *refs):
+    ins, w_hbm, final = refs[:4], refs[4:11], refs[11]
+    scratch = refs[12:]
+    regrid_scratch, rest = scratch[:20], scratch[20:]
+    padded, w_vmem, w_sem, unet_scratch = rest[0], rest[1:8], rest[8], rest[9:]
+    copies = [pltpu.make_async_copy(a, b, w_sem.at[i]) for i, (a, b) in enumerate(zip(w_hbm, w_vmem))]
+    regrid_kernel(tile_rows, tile_cols, copies, *ins, padded, *regrid_scratch)
+    for copy in copies:
+        copy.wait()
+    unet_kernel(tile_rows, tile_cols, padded, *w_vmem, final, *unet_scratch)
+
+
 def regrid_kernel(
-    tile_rows, tile_cols, src_in, req_in, sten_in, wgt_in, out_ref,
+    tile_rows, tile_cols, weight_copies, src_in, req_in, sten_in, wgt_in, out_ref,
     src_ref, req_ref, sten_ref, wgt_ref, load, reqs, src_t, mix, outbox, inbox, acc, pad, slot_rows, weight_rows,
     req_send, req_recv, box_send, box_recv, halo_send, halo_recv,
 ):
@@ -221,6 +222,8 @@
         )
     ]
     for copy in loads:
+        copy.start()
+    for copy in weight_copies:
         copy.start()
 
     barrier = pltpu.get_barrier_semaphore()
@@ -439,7 +442,7 @@
         post(step, me).wait_send()
 
 
-def regrid(source, wanted, stencil, weight, tile_rows, tile_cols):
+def regrid(source, wanted, stencil, weight, weights, tile_rows, tile_cols):
     f32, bf16 = jnp.float32, jnp.bfloat16
     n, cap = wanted.shape
     cells, columns = source.shape
@@ -448,9 +451,9 @@
     rows = tile_rows + 2 * HALO
     dma = pltpu.SemaphoreType.DMA
     return pl.pallas_call(
-        functools.partial(regrid_kernel, tile_rows, tile_cols),
-        out_shape=jax.ShapeDtypeStruct((rows * (tile_cols + 2 * HALO), columns), bf16),
-        in_specs=[pl.BlockSpec(memory_space=pltpu.HBM)] * 4,
+        functools.partial(whole_kernel, tile_rows, tile_cols),
+        out_shape=jax.ShapeDtypeStruct((tile_rows * tile_cols, columns), bf16),
+        in_specs=[pl.BlockSpec(memory_space=pltpu.HBM)] * 11,
         out_specs=pl.BlockSpec(memory_space=pltpu.VMEM),
         scratch_shapes=[
             pltpu.VMEM(source.shape, bf16),
@@ -468,28 +471,29 @@
             pltpu.VMEM((stencil.shape[1], spots), f32),
             pltpu.VMEM((stencil.shape[1], spots), f32),
             dma((n,)), dma((n,)), dma((n,)), dma((n,)), dma((8,)), dma((8,)),
-        ],
+            pltpu.VMEM((rows * (tile_cols + 2 * HALO), columns), bf16),
+        ] + [pltpu.VMEM(w.shape, bf16) for w in weights] + [dma((7,))] + unet_scratch(tile_rows, tile_cols),
         compiler_params=pltpu.CompilerParams(
-            collective_id=0, has_side_effects=True, vmem_limit_bytes=56 * 1024 * 1024
+            collective_id=0, has_side_effects=True, vmem_limit_bytes=60 * 1024 * 1024
         ),
         cost_estimate=pl.CostEstimate(
             flops=10**9, bytes_accessed=2 * 10**6, transcendentals=0
         ),
-    )(source, wanted, stencil, weight)
+    )(source, wanted, stencil, weight, *weights)
 
 
 def body(source_tiles, requests, stencil, regrid_weight, *weights):
     tile_rows, tile_cols = stencil.shape[:2]
     cells, columns = source_tiles.shape[2:]
-    padded = regrid(
+    result = regrid(
         source_tiles.reshape(cells, columns),
         requests.reshape(requests.shape[2:]),
         stencil.transpose(0, 2, 1),
         regrid_weight.transpose(0, 2, 1),
+        (*weights[:-1], weights[-1].T),
         tile_rows,
         tile_cols,
     )
-    result = unet(padded, tile_rows, tile_cols, weights)
     return result.reshape(tile_rows, tile_cols, 2, FIELDS)
 
 

time: 37.5 us -> 37.3 us (level)
    unnamed x16 -> x0, local copies, waits for them, and re-layouts: 1.08 us -> none
    reshape x1, local copies, waits for them, and re-layouts: 1.06 us -> 2 us  [body(): return result.reshape(tile_rows, tile_cols, 2, FIELDS)]
    pallas_call x2 -> x1, Pallas kernels: 35.1 us -> 35.1 us  [regrid(): pl.pallas_call(functools.partial(whole_kernel, tile_rows, tile_cols), out...]
where the time goes in v1:
time: 37.3 us; the launch traced here: 37.1 us
  Pallas kernels  35.1 us (94%)
  local copies, waits for them, and re-layouts  2 us (5%)
    pallas_call x1, Pallas kernels, regrid(): pl.pallas_call(functools.partial(whole_kernel, tile_rows, tile_cols), out...  35.1 us
    reshape x1, local copies, waits for them, and re-layouts, body(): return result.reshape(tile_rows, tile_cols, 2, FIELDS)  2 us

profile of v1, /device:TPU:0, one launch (start us, length us, event | category | flops | bytes accessed | tf_op | source)
XLA Modules:
  0.0 37.1 jit_solution(16751813037571335343)
XLA Ops:
  0.0 35.1 %shard_map.109 = bf16[1024,128]{1,0:T(8,128)(2,1)} custom-call(bf16[1024,128]{1,0:T(8,128)(2,1)} %bitcast.5, s32[8,256]{1,0:T(8,128)} %bitcast.9, s32[32,4,32]{2,1,0:T(4,128)} %bitcast.6, f32[32,4,32]{2,1,0:T(4,128)} %bitcast.7, bf16[3,3,64,128]{3,2,1,0:T(8,128)(2,1)} %refs_4_.1, bf16[3,3,128,128]{3,2,1,0:T(8,128)(2,1)} %refs_5_.1, ...), custom_call_target="tpu_custom_call" | custom-call | flops 1000000000 | bytes 2000000 | tf_op jit(solution)/shard_map/pallas_call | solution.py:453
  35.1 2.0 %reshape.11 = bf16[32,32,2,64]{3,2,1,0:T(2,128)(2,1)} reshape(bf16[1024,128]{1,0:T(8,128)(2,1)} %shard_map.109) | data formatting | bytes 524288 | tf_op jit(solution)/shard_map/reshape | solution.py:497

commit v2 on v1

v2 whole, which is shorter than its diff:
```python
import functools

import jax
import jax.numpy as jnp
from jax import lax
from jax.experimental import pallas as pl
from jax.experimental.pallas import tpu as pltpu
from jax.sharding import PartitionSpec as P

FIELDS = 64
CH = 128
HALO = 8
f32, bf16 = jnp.float32, jnp.bfloat16
MESH = pl.DeviceIdType.MESH


def silu(a):
    return a * (0.5 + 0.5 * jnp.tanh(0.5 * a))


def pair_weight(out, base, w, dy):
    zero = jnp.zeros((CH, CH), bf16)
    rows = [
        (w[dy, 1], w[dy, 0]), (w[dy, 2], w[dy, 1]), (w[dy, 0], zero), (zero, w[dy, 2])
    ]
    for i, (even, odd) in enumerate(rows):
        place = slice(base + i * CH, base + (i + 1) * CH)
        out[place, :CH] = even
        out[place, CH:] = odd


def prepare(w_in, w_enc, w_m1, w_m2, w_d1, w_d2, w_out, c_in, c_enc, c_m1, c_m2, c_d1, c_d2, c_out):
    quad = 4 * FIELDS
    none = jnp.zeros((FIELDS, CH), bf16)
    for dy in range(3):
        for j in range(4):
            place = slice(dy * quad + j * FIELDS, dy * quad + (j + 1) * FIELDS)
            c_in[place, :CH] = w_in[dy, j] if j < 3 else none
            c_in[place, CH:] = w_in[dy, j - 1] if j > 0 else none
        base = dy * 4 * CH
        pair_weight(c_enc, base, w_enc, dy)
        pair_weight(c_m1, base, w_m1, dy)
        pair_weight(c_m2, base, w_m2, dy)
        pair_weight(c_d2, base, w_d2, dy)
        for par in range(2):
            pair_weight(c_d1.at[par], base, w_d1.at[:, :, CH:], dy)
    zero = jnp.zeros((CH, CH), bf16)
    for par in range(2):
        groups = ((0, 1), (2,)) if par == 0 else ((0,), (1, 2))
        for g, dys in enumerate(groups):
            taps = [sum(w_d1[dy, dx, :CH].astype(f32) for dy in dys) for dx in range(3)]
            base = 12 * CH + g * 3 * CH
            rows = [
                (taps[0].astype(bf16), zero),
                ((taps[1] + taps[2]).astype(bf16), (taps[0] + taps[1]).astype(bf16)),
                (zero, taps[2].astype(bf16)),
            ]
            for i, (even, odd) in enumerate(rows):
                place = slice(base + i * CH, base + (i + 1) * CH)
                c_d1[par, place, :CH] = even
                c_d1[par, place, CH:] = odd
    last = w_out[...].astype(f32).T.astype(bf16)
    pad = jnp.zeros((CH, CH - FIELDS), bf16)
    full = jnp.concatenate([last.astype(f32), pad.astype(f32)], axis=1).astype(bf16)
    c_out[:CH, :CH] = full
    c_out[CH:, CH:] = full
    c_out[:CH, CH:] = zero
    c_out[CH:, :CH] = zero


def pairs_of(tile_cols):
    return tile_cols // 2 + HALO


def unet_body(tile_rows, tile_cols, at_top, at_bottom, pad, weights, out_ref, quad, first, skip, tmp, pooled, middle, up, dec, last):
    c_in, c_enc, c_m1, c_m2, c_d1, c_d2, c_out = weights
    rows = tile_rows + 2 * HALO
    pairs = pairs_of(tile_cols)
    line = 2 * pairs
    half = line // 2
    h_first, h_skip = tile_rows + 14, tile_rows + 12
    h_pool = h_skip // 2
    h_mid, h_coarse = h_pool - 2, h_pool - 4
    h_dec = (tile_rows + 2) // 2
    own = tile_cols // 2
    low = lax.broadcasted_iota(jnp.int32, (1, 1, CH), 2) < FIELDS
    upper = lax.broadcasted_iota(jnp.int32, (1, 8, 1), 1) < 4
    groups = pairs // 8

    def rolled(value, by):
        return pltpu.roll(value, by % value.shape[0], 0)

    def line_up(start, count):
        columns = []
        for par in range(2):
            lanes = slice(par * CH, (par + 1) * CH)
            parts = []
            for g in range(groups):
                place = pl.ds(start * 4, count * 4)
                a = pad[2 * g, place, lanes].astype(f32).reshape(count // 2, 8, CH)
                b = pad[2 * g + 1, place, lanes].astype(f32).reshape(count // 2, 8, CH)
                turned_a, turned_b = pltpu.roll(a, 4, 1), pltpu.roll(b, 4, 1)
                both = jnp.stack(
                    [jnp.where(upper, a, turned_b), jnp.where(upper, turned_a, b)], axis=1
                )
                parts.append(both.reshape(count, 8, CH))
            columns.append(jnp.concatenate(parts, axis=1).reshape(count * pairs, CH))
        even, odd = columns
        even_t, odd_t = pltpu.roll(even, FIELDS, 1), pltpu.roll(odd, FIELDS, 1)
        before, before_t = rolled(odd, 1), rolled(odd_t, 1)
        after, after_t = rolled(even, -1), rolled(even_t, -1)
        lo = low.reshape(1, CH)
        one = [jnp.where(lo, before, even_t), jnp.where(lo, odd, after_t)]
        two = [jnp.where(lo, before_t, even), jnp.where(lo, odd_t, after)]
        both = [
            jnp.concatenate(v, axis=1).reshape(count, pairs, 2 * CH) for v in (one, two)
        ]
        value = jnp.concatenate(both, axis=1).reshape(count * line, 2 * CH).astype(bf16)
        quad[pl.ds(start * line, count * line), :] = value

    step = 16
    @pl.loop(0, rows // step)
    def _(i):
        line_up(pl.multiple_of(i * step, step), step)

    def dot(windows, weight):
        return silu(
            jnp.dot(jnp.concatenate(windows, axis=1), weight, preferred_element_type=f32)
        )

    def sides(value):
        return jnp.concatenate([rolled(value[:, CH:], 1), rolled(value[:, :CH], -1)], axis=1)

    def window(ref, start, count, width, dy):
        return ref[pl.ds(pl.multiple_of((start + dy) * width, 8), count * width), :]

    def clear(ref, depth, inner, width):
        @pl.when(at_top)
        def _():
            ref[: depth * width] = jnp.zeros((depth * width, ref.shape[1]), ref.dtype)

        @pl.when(at_bottom)
        def _():
            ref[(depth + inner) * width :] = jnp.zeros((depth * width, ref.shape[1]), ref.dtype)

    def chunks(total, count, fn):
        if total == count:
            fn(0)
        else:
            @pl.loop(0, total // count)
            def _(i):
                fn(i * count)

    count = h_first // FIRST_CHUNKS

    def first_step(start):
        v = dot([window(quad, start, count, line, dy) for dy in range(3)], c_in[...])
        v = jnp.concatenate([v, sides(v)], axis=1).astype(bf16)
        first[pl.ds(pl.multiple_of(start * line, 16), count * line), :] = v

    chunks(h_first, count, first_step)
    clear(first, 7, tile_rows, line)

    count_s = h_skip // SKIP_CHUNKS

    def skip_step(start):
        v = dot([window(first, start, count_s, line, dy) for dy in range(3)], c_enc[...])
        both = jnp.concatenate([v, sides(v)], axis=1).astype(bf16)
        skip[pl.ds(start // 2, count_s // 2)] = both.reshape(count_s // 2, 2 * line, 4 * CH)
        v = v.reshape(count_s // 2, 2 * line, 2 * CH)
        v = (v[:, :line] + v[:, line:]).reshape(count_s // 2 * line, 2 * CH)
        place = pl.ds(pl.multiple_of(start * line // 2, 8), count_s // 2 * line)
        tmp[place, :] = (v[:, :CH] + v[:, CH:]) * 0.25

    chunks(h_skip, count_s, skip_step)

    @pl.when(at_top)
    def _():
        skip[:3] = jnp.zeros((3, 2 * line, 4 * CH), bf16)

    @pl.when(at_bottom)
    def _():
        skip[h_pool - 3 :] = jnp.zeros((3, 2 * line, 4 * CH), bf16)

    @pl.when(at_top)
    def _():
        tmp[: 3 * line] = jnp.zeros((3 * line, CH), f32)

    @pl.when(at_bottom)
    def _():
        tmp[(h_pool - 3) * line :] = jnp.zeros((3 * line, CH), f32)

    size = h_pool * half
    v = jnp.concatenate([tmp[pl.ds(0, size, stride=2), :], tmp[pl.ds(1, size, stride=2), :]], axis=1)
    pooled[...] = jnp.concatenate([v, sides(v)], axis=1)

    v = dot([window(pooled, 0, h_mid, half, dy).astype(bf16) for dy in range(3)], c_m1[...])
    middle[...] = jnp.concatenate([v, sides(v)], axis=1)
    clear(middle, 2, tile_rows // 2, half)

    v = dot([window(middle, 0, h_coarse, half, dy).astype(bf16) for dy in range(3)], c_m2[...])
    size = h_coarse * half
    tmp[pl.ds(0, size, stride=2), :] = v[:, :CH]
    tmp[pl.ds(1, size, stride=2), :] = v[:, CH:]
    v = tmp[: 2 * size, :]
    up[...] = jnp.concatenate([rolled(v, 1), v, rolled(v, -1)], axis=1).astype(bf16)
    clear(up, 1, tile_rows // 2, line)

    def dec_step(par):
        def skip3(t, p):
            return skip[t : t + h_dec, p * line : (p + 1) * line, :].reshape(h_dec * line, 4 * CH)

        if par == 0:
            windows = [skip3(2, 0), skip3(2, 1), skip3(3, 0)]
        else:
            windows = [skip3(2, 1), skip3(3, 0), skip3(3, 1)]
        windows += [window(up, 0, h_dec, line, d) for d in range(2)]
        v = dot(windows, c_d1[par])

        def compact(value):
            value = value.reshape(h_dec, 2, groups, 8, value.shape[1])
            turned = [pltpu.roll(value[:, :, g].reshape(h_dec * 2, 8, -1), 4, 1) for g in range(groups)]
            parts = [
                jnp.where(upper, turned[g], turned[g + 1]).reshape(h_dec, 2, 8, -1)
                for g in range(groups - 1)
            ]
            return jnp.concatenate(parts, axis=2).reshape(h_dec, 2 * own, -1)

        both = jnp.concatenate([compact(v), compact(sides(v))], axis=2)
        dec[:, par * 2 * own : (par + 1) * 2 * own, :] = both.astype(bf16)

    dec_step(0)
    dec_step(1)

    @pl.when(at_top)
    def _():
        dec[0, : 2 * own] = jnp.zeros((2 * own, 4 * CH), bf16)

    @pl.when(at_bottom)
    def _():
        dec[h_dec - 1, 2 * own :] = jnp.zeros((2 * own, 4 * CH), bf16)

    n = tile_rows // 2

    def last_step(py):
        windows = [
            dec[d // 2 : d // 2 + n, d % 2 * 2 * own : (d % 2 + 1) * 2 * own, :].reshape(n * 2 * own, 4 * CH)
            for d in range(py, py + 3)
        ]
        v = dot(windows, c_d2[...])
        z = jnp.dot(v.astype(bf16), c_out[...], preferred_element_type=f32)
        z = z.reshape(n, 2 * own, 2 * CH)
        for px in range(2):
            for b in range(2):
                piece = z[:, b * own : (b + 1) * own, px * CH : (px + 1) * CH]
                last[:, pl.ds(py * 4 * own + 2 * px + b, own, stride=4), :] = piece

    last_step(0)
    last_step(1)
    out_ref[...] = last[...].reshape(n * 8 * own, CH)[:, :FIELDS].astype(bf16)


FIRST_CHUNKS, SKIP_CHUNKS, DEC_CHUNKS = 2, 2, 2


def unet_scratch(tile_rows, tile_cols):
    line = 2 * pairs_of(tile_cols)
    half = line // 2
    h_pool = (tile_rows + 12) // 2
    return [
        pltpu.VMEM(((tile_rows + 2 * HALO) * line, 2 * CH), bf16),
        pltpu.VMEM(((tile_rows + 14) * line, 4 * CH), bf16),
        pltpu.VMEM((h_pool, 2 * line, 4 * CH), bf16),
        pltpu.VMEM((h_pool * line, CH), f32),
        pltpu.VMEM((h_pool * half, 4 * CH), f32),
        pltpu.VMEM(((h_pool - 2) * half, 4 * CH), f32),
        pltpu.VMEM(((h_pool - 4) * line, 3 * CH), bf16),
        pltpu.VMEM((tile_rows // 2 + 1, 2 * tile_cols, 4 * CH), bf16),
        pltpu.VMEM((tile_rows // 2, 4 * tile_cols, CH), f32),
    ]


def weight_scratch():
    square = pltpu.VMEM((12 * CH, 2 * CH), bf16)
    return [
        pltpu.VMEM((12 * FIELDS, 2 * CH), bf16), square, square, square,
        pltpu.VMEM((2, 18 * CH, 2 * CH), bf16), square, pltpu.VMEM((2 * CH, 2 * CH), bf16),
    ]


def whole_kernel(tile_rows, tile_cols, *refs):
    ins, w_hbm, final, scratch = refs[:4], refs[4:11], refs[11], refs[12:]
    w_vmem, w_sem, mats = scratch[:7], scratch[7], scratch[8:15]
    pad, own, unet_refs = scratch[15], scratch[16:36], scratch[36:]

    def weights_start():
        for i in range(7):
            pltpu.make_async_copy(w_hbm[i], w_vmem[i], w_sem.at[i]).start()

    def weights_ready():
        for i in range(7):
            pltpu.make_async_copy(w_hbm[i], w_vmem[i], w_sem.at[i]).wait()
        prepare(*w_vmem, *mats)

    regrid_body(tile_rows, tile_cols, weights_start, weights_ready, *ins, pad, *own)
    row = lax.axis_index("row")
    unet_body(
        tile_rows, tile_cols, row == 0, row == lax.axis_size("row") - 1, pad, mats, final, *unet_refs
    )


def regrid_body(
    tile_rows, tile_cols, weights_start, weights_ready, src_in, req_in, sten_in, wgt_in, pad,
    src_ref, req_ref, sten_ref, wgt_ref, load, asks, reqs, src_t, mix, outbox, inbox, acc, slot_rows, weight_rows,
    req_send, req_recv, box_send, box_recv, halo_send, halo_recv,
):
    row, me = lax.axis_index("row"), lax.axis_index("col")
    n_row, n = lax.axis_size("row"), lax.axis_size("col")
    cap = req_ref.shape[1]
    cells = src_ref.shape[0]
    spots = tile_rows * tile_cols
    has_up, has_down = row > 0, row < n_row - 1
    wide = HALO // 2
    blocks = tile_cols // HALO
    edge = HALO * wide
    inner = tile_rows * wide

    loads = [
        pltpu.make_async_copy(outer, held, load.at[i])
        for i, (outer, held) in enumerate(
            [(req_in, req_ref), (src_in, src_ref), (sten_in, sten_ref), (wgt_in, wgt_ref)]
        )
    ]
    for copy in loads:
        copy.start()

    barrier = pltpu.get_barrier_semaphore()

    def greet(r, c):
        pl.semaphore_signal(
            barrier, inc=1, device_id=(r, lax.rem(c + n, n)), device_id_type=MESH
        )

    @pl.loop(1, n)
    def _(step):
        greet(row, me + step)

    @pl.when(has_up)
    def _():
        for d in (-1, 0, 1):
            greet(row - 1, me + d)

    @pl.when(has_down)
    def _():
        for d in (-1, 0, 1):
            greet(row + 1, me + d)

    weights_start()
    loads[0].wait()
    parts = cap // CH
    for j in range(n):
        for part in range(parts):
            asks[j, part : part + 1, :] = req_ref[j : j + 1, part * CH : (part + 1) * CH]

    rows_beside = jnp.minimum(row, 1) + jnp.minimum(n_row - 1 - row, 1)
    pl.semaphore_wait(barrier, n - 1 + 3 * rows_beside)

    def ask(step, sender):
        dest = lax.rem(me + step, n)
        return pltpu.make_async_remote_copy(
            src_ref=asks.at[dest],
            dst_ref=reqs.at[sender],
            send_sem=req_send.at[step],
            recv_sem=req_recv.at[sender],
            device_id=(row, dest),
            device_id_type=MESH,
        )

    @pl.loop(1, n)
    def _(step):
        ask(step, me).start()

    reqs[me] = asks[me]
    loads[1].wait()
    src_t[...] = src_ref[...].astype(f32).T.astype(bf16)

    loads[2].wait()
    loads[3].wait()
    taps = sten_ref.shape[0] // tile_rows
    lane = lax.broadcasted_iota(jnp.int32, (tile_cols, spots), 1)
    cell = lax.broadcasted_iota(jnp.int32, (tile_cols, spots), 0)
    column = lane // (spots // 2) + lane % wide * 2 + lane // inner % blocks * HALO
    turn = jnp.where(cell == column, 1.0, 0.0).astype(bf16)
    held = tile_rows * taps
    mine = lax.broadcasted_iota(jnp.int32, (held, spots), 0) // taps == (
        lax.broadcasted_iota(jnp.int32, (held, spots), 1) // wide % tile_rows
    )

    def in_order(values):
        spread = jnp.dot(values.astype(bf16), turn, preferred_element_type=f32)
        spread = jnp.where(mine, spread, 0.0).reshape(held // 8, 8, spots)
        total = jnp.sum(spread, axis=0)
        return total[:taps] + total[taps:]

    slots = sten_ref[...]
    slot_rows[...] = in_order((slots // 256).astype(f32)) * 256.0 + in_order((slots % 256).astype(f32))
    weight_rows[...] = in_order(wgt_ref[...])
    tile, piece = 16, 256

    def ladder(width):
        return lax.broadcasted_iota(jnp.int32, (tile, width), 0).astype(f32).astype(bf16)

    def spread(values):
        return jnp.broadcast_to(values, (tile, values.shape[1])).astype(bf16)

    lanes = min(512, spots)
    zero, one = jnp.zeros((), bf16), jnp.ones((), bf16)

    def mix_block(j):
        for left_lane in range(0, spots, lanes):
            here = slice(left_lane, left_lane + lanes)
            ids = ladder(lanes)
            weights = [spread(weight_rows[k : k + 1, here]) for k in range(taps)]
            for start in range(0, cap, piece):
                base = (j * cap + start).astype(f32)
                near = [spread(slot_rows[k : k + 1, here] - base) for k in range(taps)]
                for g in range(0, min(piece, cap), tile):
                    step_ids = ids + jnp.asarray(g, bf16)
                    total = None
                    for k in range(taps):
                        part = jnp.where(step_ids == near[k], weights[k], zero)
                        total = part if total is None else total + part
                    mix[j, start + g : start + g + tile, here] = total

    @pl.loop(0, n // 2)
    def _(j):
        mix_block(j)

    def picked(dest):
        asked = jnp.concatenate(
            [reqs[dest, part : part + 1, :] for part in range(parts)], axis=1
        ).astype(f32)
        ids = ladder(cap)
        rows = []
        for start in range(0, cells, piece):
            near = spread(asked - float(start))
            for g in range(0, piece, tile):
                rows.append(jnp.where(ids + jnp.asarray(g, bf16) == near, one, zero))
        hot = jnp.concatenate(rows, axis=0)
        return jnp.dot(src_t[...], hot, preferred_element_type=f32).astype(bf16)

    def post(step, sender):
        return pltpu.make_async_remote_copy(
            src_ref=outbox.at[step],
            dst_ref=inbox.at[sender],
            send_sem=box_send.at[step],
            recv_sem=box_recv.at[sender],
            device_id=(row, lax.rem(me + step, n)),
            device_id_type=MESH,
        )

    @pl.loop(1, n)
    def _(step):
        dest = lax.rem(me + step, n)
        ask(step, dest).wait_recv()
        outbox[step] = picked(dest)
        post(step, me).start()

    inbox[me] = picked(me)

    @pl.loop(n // 2, n)
    def _(j):
        mix_block(j)

    acc[...] = jnp.dot(inbox[me], mix[me], preferred_element_type=f32)
    weights_ready()

    @pl.loop(1, n)
    def _(step):
        sender = lax.rem(me - step + n, n)
        post(step, sender).wait_recv()
        acc[...] += jnp.dot(inbox[sender], mix[sender], preferred_element_type=f32)

    for par in range(2):
        turned = acc[:, par * spots // 2 : (par + 1) * spots // 2].T.astype(bf16)
        lanes_here = slice(par * CH, (par + 1) * CH)
        for xb in range(blocks):
            pad[xb + 1, edge : edge + inner, lanes_here] = turned[xb * inner : (xb + 1) * inner]

    @pl.when(jnp.logical_not(has_up))
    def _():
        pad[:, :edge] = jnp.zeros((blocks + 2, edge, 2 * CH), bf16)

    @pl.when(jnp.logical_not(has_down))
    def _():
        pad[:, edge + inner :] = jnp.zeros((blocks + 2, edge, 2 * CH), bf16)

    mid = slice(edge, edge + inner)
    first, last = slice(edge, 2 * edge), slice(inner, inner + edge)
    low, high = slice(0, edge), slice(edge + inner, 2 * edge + inner)
    every = slice(1, blocks + 1)
    left, right = slice(1, 2), slice(blocks, blocks + 1)
    before, after = slice(0, 1), slice(blocks + 1, blocks + 2)
    moves = [
        (0, 1, (right, mid), (before, mid)),
        (0, -1, (left, mid), (after, mid)),
        (1, 0, (every, last), (every, low)),
        (1, 1, (right, last), (before, low)),
        (1, -1, (left, last), (after, low)),
        (-1, 0, (every, first), (every, high)),
        (-1, 1, (right, first), (before, high)),
        (-1, -1, (left, first), (after, high)),
    ]

    def shift(i):
        dr, dc, src, dst = moves[i]
        return pltpu.make_async_remote_copy(
            src_ref=pad.at[src[0], src[1]],
            dst_ref=pad.at[dst[0], dst[1]],
            send_sem=halo_send.at[i],
            recv_sem=halo_recv.at[i],
            device_id=(row + dr, lax.rem(me + dc + n, n)),
            device_id_type=MESH,
        )

    @pl.when(has_down)
    def _():
        for i in (2, 3, 4):
            shift(i).start()

    @pl.when(has_up)
    def _():
        for i in (5, 6, 7):
            shift(i).start()

    for i in (0, 1):
        shift(i).start()

    @pl.loop(1, n)
    def _(step):
        ask(step, me).wait_send()
        post(step, me).wait_send()

    for i in (0, 1):
        shift(i).wait()

    @pl.when(has_up)
    def _():
        for i in (2, 3, 4):
            shift(i).wait_recv()

    @pl.when(has_down)
    def _():
        for i in (5, 6, 7):
            shift(i).wait_recv()

    @pl.when(has_down)
    def _():
        for i in (2, 3, 4):
            shift(i).wait_send()

    @pl.when(has_up)
    def _():
        for i in (5, 6, 7):
            shift(i).wait_send()


def forward(source, wanted, stencil, weight, weights, tile_rows, tile_cols):
    n, cap = wanted.shape
    cells, columns = source.shape
    spots = tile_rows * tile_cols
    blocks = tile_cols // HALO
    rows = tile_rows + 2 * HALO
    taps = stencil.shape[0] // tile_rows
    dma = pltpu.SemaphoreType.DMA
    return pl.pallas_call(
        functools.partial(whole_kernel, tile_rows, tile_cols),
        out_shape=jax.ShapeDtypeStruct((2 * spots, FIELDS), bf16),
        in_specs=[pl.BlockSpec(memory_space=pltpu.HBM)] * 11,
        out_specs=pl.BlockSpec(memory_space=pltpu.VMEM),
        scratch_shapes=[pltpu.VMEM(w.shape, bf16) for w in weights]
        + [dma((7,))]
        + weight_scratch()
        + [
            pltpu.VMEM((blocks + 2, rows * HALO // 2, 2 * columns), bf16),
            pltpu.VMEM(source.shape, bf16),
            pltpu.VMEM(wanted.shape, jnp.int32),
            pltpu.VMEM(stencil.shape, jnp.int32),
            pltpu.VMEM(weight.shape, f32),
            dma((4,)),
            pltpu.VMEM((n, cap // CH, CH), jnp.int32),
            pltpu.VMEM((n, cap // CH, CH), jnp.int32),
            pltpu.VMEM((columns, cells), bf16),
            pltpu.VMEM((n, cap, spots), bf16),
            pltpu.VMEM((n, columns, cap), bf16),
            pltpu.VMEM((n, columns, cap), bf16),
            pltpu.VMEM((columns, spots), f32),
            pltpu.VMEM((taps, spots), f32),
            pltpu.VMEM((taps, spots), f32),
            dma((n,)), dma((n,)), dma((n,)), dma((n,)), dma((8,)), dma((8,)),
        ]
        + unet_scratch(tile_rows, tile_cols),
        compiler_params=pltpu.CompilerParams(
            collective_id=0, has_side_effects=True, vmem_limit_bytes=60 * 1024 * 1024
        ),
        cost_estimate=pl.CostEstimate(
            flops=10**9, bytes_accessed=2 * 10**6, transcendentals=0
        ),
    )(source, wanted, stencil, weight, *weights)


def body(source_tiles, requests, stencil, regrid_weight, *weights):
    tile_rows, tile_cols, taps = stencil.shape
    cells, columns = source_tiles.shape[2:]
    result = forward(
        source_tiles.reshape(cells, columns),
        requests.reshape(requests.shape[2:]),
        stencil.transpose(0, 2, 1).reshape(tile_rows * taps, tile_cols),
        regrid_weight.transpose(0, 2, 1).reshape(tile_rows * taps, tile_cols),
        (*weights[:-1], weights[-1].T),
        tile_rows,
        tile_cols,
    )
    return result.reshape(tile_rows, tile_cols, 2, FIELDS)


def solution(mesh):
    placed = (P("row", "col", None, None),) * 2 + (P("row", "col", None),) * 2 + (P(),) * 7
    return jax.shard_map(
        body, mesh=mesh, in_specs=placed, out_specs=P("row", "col", None, None), check_vma=False
    )
```

time: 37.3 us -> 34.6 us (0.928)
  Pallas kernels: 35.1 us -> 32.1 us
    pallas_call x1, Pallas kernels: 35.1 us -> 32.1 us  [forward(): pl.pallas_call(functools.partial(whole_kernel, tile_rows, tile_cols), out...]
    unnamed x0 -> x1, local copies, waits for them, and re-layouts: none -> 2.28 us
    reshape x1 -> x0, local copies, waits for them, and re-layouts: 2 us -> none  [body(): return result.reshape(tile_rows, tile_cols, 2, FIELDS)]
where the time goes in v2:
time: 34.6 us; the launch traced here: 34.4 us
  Pallas kernels  32.1 us (93%)
  local copies, waits for them, and re-layouts  2.28 us (7%)
    pallas_call x1, Pallas kernels, forward(): pl.pallas_call(functools.partial(whole_kernel, tile_rows, tile_cols), out...  32.1 us
    unnamed x1, local copies, waits for them, and re-layouts  2.28 us

profile of v2, /device:TPU:0, one launch (start us, length us, event | category | flops | bytes accessed | tf_op | source)
XLA Modules:
  0.0 34.4 jit_solution(2806012157005523918)
XLA Ops:
  0.0 32.1 %shard_map.109 = bf16[2048,64]{1,0:T(8,128)(2,1)} custom-call(bf16[1024,128]{1,0:T(8,128)(2,1)} %bitcast.11, s32[8,256]{1,0:T(8,128)} %bitcast.15, s32[128,32]{1,0:T(8,128)} %bitcast.12, f32[128,32]{1,0:T(8,128)} %bitcast.13, bf16[3,3,64,128]{3,2,1,0:T(8,128)(2,1)} %refs_4_.1, bf16[3,3,128,128]{3,2,1,0:T(8,128)(2,1)} %refs_5_.1, ...), custom_call_target="tpu_custom_call" | custom-call | flops 1000000000 | bytes 2000000 | tf_op jit(solution)/shard_map/pallas_call | solution.py:576
  32.1 2.3 %copy.13 = bf16[32,32,2,64]{3,2,1,0:T(2,128)(2,1)} copy(bf16[32,32,2,64]{3,2,1,0:T(2,128)(2,1)} %bitcast.10) | data formatting | bytes 524288

commit v3 on v2

--- a/solution.py
+++ b/solution.py
@@ -72,8 +72,8 @@
     return tile_cols // 2 + HALO
 
 
-def unet_body(tile_rows, tile_cols, at_top, at_bottom, pad, weights, out_ref, quad, first, skip, tmp, pooled, middle, up, dec, last):
-    c_in, c_enc, c_m1, c_m2, c_d1, c_d2, c_out = weights
+def unet_body(tile_rows, tile_cols, at_top, at_bottom, pad, weights, dec, quad, first, skip, tmp, pooled, middle, up):
+    c_in, c_enc, c_m1, c_m2, c_d1 = weights
     rows = tile_rows + 2 * HALO
     pairs = pairs_of(tile_cols)
     line = 2 * pairs
@@ -227,40 +227,42 @@
             return jnp.concatenate(parts, axis=2).reshape(h_dec, 2 * own, -1)
 
         both = jnp.concatenate([compact(v), compact(sides(v))], axis=2)
-        dec[:, par * 2 * own : (par + 1) * 2 * own, :] = both.astype(bf16)
+        both = both.astype(bf16)
+        for i in range(h_dec):
+            dec[2 * i + par] = both[i]
 
     dec_step(0)
     dec_step(1)
 
     @pl.when(at_top)
     def _():
-        dec[0, : 2 * own] = jnp.zeros((2 * own, 4 * CH), bf16)
+        dec[0] = jnp.zeros((2 * own, 4 * CH), bf16)
 
     @pl.when(at_bottom)
     def _():
-        dec[h_dec - 1, 2 * own :] = jnp.zeros((2 * own, 4 * CH), bf16)
-
-    n = tile_rows // 2
-
-    def last_step(py):
+        dec[2 * h_dec - 1] = jnp.zeros((2 * own, 4 * CH), bf16)
+
+
+def tail_body(tile_rows, own, dec, c_d2, c_out, last, put):
+    n = tile_rows // TAIL_CHUNKS
+    for i in range(TAIL_CHUNKS):
         windows = [
-            dec[d // 2 : d // 2 + n, d % 2 * 2 * own : (d % 2 + 1) * 2 * own, :].reshape(n * 2 * own, 4 * CH)
-            for d in range(py, py + 3)
+            dec[i * n + dy : (i + 1) * n + dy].reshape(n * 2 * own, 4 * CH) for dy in range(3)
         ]
-        v = dot(windows, c_d2[...])
+        v = silu(
+            jnp.dot(jnp.concatenate(windows, axis=1), c_d2[...], preferred_element_type=f32)
+        )
         z = jnp.dot(v.astype(bf16), c_out[...], preferred_element_type=f32)
         z = z.reshape(n, 2 * own, 2 * CH)
         for px in range(2):
             for b in range(2):
                 piece = z[:, b * own : (b + 1) * own, px * CH : (px + 1) * CH]
-                last[:, pl.ds(py * 4 * own + 2 * px + b, own, stride=4), :] = piece
-
-    last_step(0)
-    last_step(1)
-    out_ref[...] = last[...].reshape(n * 8 * own, CH)[:, :FIELDS].astype(bf16)
-
-
-FIRST_CHUNKS, SKIP_CHUNKS, DEC_CHUNKS = 2, 2, 2
+                last[pl.ds(i * n * own * 4 + 2 * px + b, n * own, stride=4), :] = piece.reshape(n * own, CH)
+        put(i * n * own * 4, n * own * 4)
+
+
+TAIL_CHUNKS = 2
+FIRST_CHUNKS, SKIP_CHUNKS = 2, 2
 
 
 def unet_scratch(tile_rows, tile_cols):
@@ -275,8 +277,6 @@
         pltpu.VMEM((h_pool * half, 4 * CH), f32),
         pltpu.VMEM(((h_pool - 2) * half, 4 * CH), f32),
         pltpu.VMEM(((h_pool - 4) * line, 3 * CH), bf16),
-        pltpu.VMEM((tile_rows // 2 + 1, 2 * tile_cols, 4 * CH), bf16),
-        pltpu.VMEM((tile_rows // 2, 4 * tile_cols, CH), f32),
     ]
 
 
@@ -284,14 +284,15 @@
     square = pltpu.VMEM((12 * CH, 2 * CH), bf16)
     return [
         pltpu.VMEM((12 * FIELDS, 2 * CH), bf16), square, square, square,
-        pltpu.VMEM((2, 18 * CH, 2 * CH), bf16), square, pltpu.VMEM((2 * CH, 2 * CH), bf16),
+        pltpu.VMEM((2, 18 * CH, 2 * CH), bf16),
     ]
 
 
 def whole_kernel(tile_rows, tile_cols, *refs):
-    ins, w_hbm, final, scratch = refs[:4], refs[4:11], refs[11], refs[12:]
-    w_vmem, w_sem, mats = scratch[:7], scratch[7], scratch[8:15]
-    pad, own, unet_refs = scratch[15], scratch[16:36], scratch[36:]
+    ins, w_hbm, outs, scratch = refs[:4], refs[4:11], refs[11:14], refs[14:]
+    w_vmem, w_sem, mats = scratch[:7], scratch[7], scratch[8:13]
+    pad, own, unet_refs = scratch[13], scratch[14:34], scratch[34:]
+    dec, c_d2, c_out = outs
 
     def weights_start():
         for i in range(7):
@@ -300,13 +301,48 @@
     def weights_ready():
         for i in range(7):
             pltpu.make_async_copy(w_hbm[i], w_vmem[i], w_sem.at[i]).wait()
-        prepare(*w_vmem, *mats)
+        prepare(*w_vmem, *mats, c_d2, c_out)
 
     regrid_body(tile_rows, tile_cols, weights_start, weights_ready, *ins, pad, *own)
     row = lax.axis_index("row")
     unet_body(
-        tile_rows, tile_cols, row == 0, row == lax.axis_size("row") - 1, pad, mats, final, *unet_refs
+        tile_rows, tile_cols, row == 0, row == lax.axis_size("row") - 1, pad, mats, dec, *unet_refs
     )
+
+
+def tail_kernel(tile_rows, own, dec, c_d2, c_out, out_ref, last, staged, sem):
+    copies = []
+
+    def put(start, count):
+        place = slice(start, start + count)
+        staged[place, :] = last[place, :FIELDS].astype(bf16)
+        copy = pltpu.make_async_copy(staged.at[place], out_ref.at[place], sem.at[len(copies)])
+        copy.start()
+        copies.append(copy)
+
+    tail_body(tile_rows, own, dec, c_d2, c_out, last, put)
+    for copy in copies:
+        copy.wait()
+
+
+def tail(dec, c_d2, c_out):
+    tile_rows, tile_cols = dec.shape[0] - 2, dec.shape[1]
+    cells = 2 * tile_rows * tile_cols
+    return pl.pallas_call(
+        functools.partial(tail_kernel, tile_rows, tile_cols // 2),
+        out_shape=jax.ShapeDtypeStruct((cells, FIELDS), bf16),
+        in_specs=[pl.BlockSpec(memory_space=pltpu.VMEM)] * 3,
+        out_specs=pl.BlockSpec(memory_space=pltpu.HBM),
+        scratch_shapes=[
+            pltpu.VMEM((cells, CH), f32),
+            pltpu.VMEM((cells, FIELDS), bf16),
+            pltpu.SemaphoreType.DMA((TAIL_CHUNKS,)),
+        ],
+        compiler_params=pltpu.CompilerParams(vmem_limit_bytes=16 * 1024 * 1024),
+        cost_estimate=pl.CostEstimate(
+            flops=10**9, bytes_accessed=2 * 10**6, transcendentals=0
+        ),
+    )(dec, c_d2, c_out)
 
 
 def regrid_body(
@@ -575,9 +611,12 @@
     dma = pltpu.SemaphoreType.DMA
     return pl.pallas_call(
         functools.partial(whole_kernel, tile_rows, tile_cols),
-        out_shape=jax.ShapeDtypeStruct((2 * spots, FIELDS), bf16),
+        out_shape=[
+            pltpu.VMEM(shape, bf16)
+            for shape in ((tile_rows + 2, tile_cols, 4 * CH), (12 * CH, 2 * CH), (2 * CH, 2 * CH))
+        ],
         in_specs=[pl.BlockSpec(memory_space=pltpu.HBM)] * 11,
-        out_specs=pl.BlockSpec(memory_space=pltpu.VMEM),
+        out_specs=[pl.BlockSpec(memory_space=pltpu.VMEM)] * 3,
         scratch_shapes=[pltpu.VMEM(w.shape, bf16) for w in weights]
         + [dma((7,))]
         + weight_scratch()
@@ -601,18 +640,18 @@
         ]
         + unet_scratch(tile_rows, tile_cols),
         compiler_params=pltpu.CompilerParams(
-            collective_id=0, has_side_effects=True, vmem_limit_bytes=60 * 1024 * 1024
+            collective_id=0, has_side_effects=True, vmem_limit_bytes=40 * 1024 * 1024
         ),
         cost_estimate=pl.CostEstimate(
             flops=10**9, bytes_accessed=2 * 10**6, transcendentals=0
         ),
-    )(source, wanted, stencil, weight, *weights)
+    )(*[pltpu.with_memory_space_constraint(a, pltpu.HBM) for a in (source, wanted, stencil, weight, *weights)])
 
 
 def body(source_tiles, requests, stencil, regrid_weight, *weights):
     tile_rows, tile_cols, taps = stencil.shape
     cells, columns = source_tiles.shape[2:]
-    result = forward(
+    done = forward(
         source_tiles.reshape(cells, columns),
         requests.reshape(requests.shape[2:]),
         stencil.transpose(0, 2, 1).reshape(tile_rows * taps, tile_cols),
@@ -621,7 +660,7 @@
         tile_rows,
         tile_cols,
     )
-    return result.reshape(tile_rows, tile_cols, 2, FIELDS)
+    return tail(*done).reshape(tile_rows, tile_cols, 2, FIELDS)
 
 
 def solution(mesh):

time: 34.6 us -> 32.2 us (0.931)
  local copies, waits for them, and re-layouts: 2.28 us -> 0 us
    pallas_call x1, Pallas kernels: 32.1 us -> 29.2 us  [forward(): pl.pallas_call(functools.partial(whole_kernel, tile_rows, tile_cols), out...]
    pallas_call x0 -> x1, Pallas kernels: none -> 2.8 us  [tail(): pl.pallas_call(functools.partial(tail_kernel, tile_rows, tile_cols // 2),...]
    unnamed x1 -> x0, local copies, waits for them, and re-layouts: 2.28 us -> none
where the time goes in v3:
time: 32.2 us; the launch traced here: 32 us
  Pallas kernels  32 us (99%)
    pallas_call x1, Pallas kernels, forward(): pl.pallas_call(functools.partial(whole_kernel, tile_rows, tile_cols), out...  29.2 us
    pallas_call x1, Pallas kernels, tail(): pl.pallas_call(functools.partial(tail_kernel, tile_rows, tile_cols // 2),...  2.8 us

profile of v3, /device:TPU:0, one launch (start us, length us, event | category | flops | bytes accessed | tf_op | source)
XLA Modules:
  0.0 32.0 jit_solution(14594135507380728360)
XLA Ops:
  0.0 29.2 %shard_map.109 = (bf16[34,32,512]{2,1,0:T(8,128)(2,1)S(1)}, bf16[1536,256]{1,0:T(8,128)(2,1)S(1)}, bf16[256,256]{1,0:T(8,128)(2,1)S(1)}) custom-call(bf16[1024,128]{1,0:T(8,128)(2,1)} %bitcast.10, s32[8,256]{1,0:T(8,128)} %bitcast.14, s32[128,32]{1,0:T(8,128)} %bitcast.11, f32[128,32]{1,0:T(8,128)} %bitcast.12, bf16[3,3,64,128]{3,2,1,0:T(8,128)(2,1)} %refs_4_.1, ...), custom_call_target="tpu_custom_call" | custom-call | flops 1000000000 | bytes 2000000 | tf_op jit(solution)/shard_map/pallas_call | solution.py:612
  29.2 2.8 %shard_map.110 = bf16[2048,64]{1,0:T(8,128)(2,1)} custom-call(bf16[34,32,512]{2,1,0:T(8,128)(2,1)S(1)} %get-tuple-element.8.dec, bf16[1536,256]{1,0:T(8,128)(2,1)S(1)} %get-tuple-element.9.c_d2, bf16[256,256]{1,0:T(8,128)(2,1)S(1)} %get-tuple-element.10.c_out), custom_call_target="tpu_custom_call" | custom-call | flops 1000000000 | bytes 2000000 | tf_op jit(solution)/shard_map/pallas_call | solution.py:331

commit v4 on v3

--- a/solution.py
+++ b/solution.py
@@ -68,11 +68,19 @@
     c_out[CH:, :CH] = zero
 
 
+def split(total, parts):
+    size = -(-total // (2 * parts)) * 2
+    return [(at, min(size, total - at)) for at in range(0, total, size)]
+
+
+FIRST_CHUNKS, SKIP_CHUNKS = 2, 2
+
+
 def pairs_of(tile_cols):
     return tile_cols // 2 + HALO
 
 
-def unet_body(tile_rows, tile_cols, at_top, at_bottom, pad, weights, dec, quad, first, skip, tmp, pooled, middle, up):
+def unet_body(tile_rows, tile_cols, at_top, at_bottom, halo_here, pad, weights, dec, quad, first, skip, tmp, pooled, middle, up):
     c_in, c_enc, c_m1, c_m2, c_d1 = weights
     rows = tile_rows + 2 * HALO
     pairs = pairs_of(tile_cols)
@@ -83,45 +91,61 @@
     h_mid, h_coarse = h_pool - 2, h_pool - 4
     h_dec = (tile_rows + 2) // 2
     own = tile_cols // 2
-    low = lax.broadcasted_iota(jnp.int32, (1, 1, CH), 2) < FIELDS
+    top_scale = jnp.where(at_top, 0.0, 1.0).astype(f32)
+    bottom_scale = jnp.where(at_bottom, 0.0, 1.0).astype(f32)
+    low = lax.broadcasted_iota(jnp.int32, (1, CH), 1) < FIELDS
     upper = lax.broadcasted_iota(jnp.int32, (1, 8, 1), 1) < 4
     groups = pairs // 8
 
     def rolled(value, by):
         return pltpu.roll(value, by % value.shape[0], 0)
 
-    def line_up(start, count):
-        columns = []
-        for par in range(2):
-            lanes = slice(par * CH, (par + 1) * CH)
-            parts = []
-            for g in range(groups):
-                place = pl.ds(start * 4, count * 4)
-                a = pad[2 * g, place, lanes].astype(f32).reshape(count // 2, 8, CH)
-                b = pad[2 * g + 1, place, lanes].astype(f32).reshape(count // 2, 8, CH)
-                turned_a, turned_b = pltpu.roll(a, 4, 1), pltpu.roll(b, 4, 1)
-                both = jnp.stack(
-                    [jnp.where(upper, a, turned_b), jnp.where(upper, turned_a, b)], axis=1
-                )
-                parts.append(both.reshape(count, 8, CH))
-            columns.append(jnp.concatenate(parts, axis=1).reshape(count * pairs, CH))
-        even, odd = columns
-        even_t, odd_t = pltpu.roll(even, FIELDS, 1), pltpu.roll(odd, FIELDS, 1)
-        before, before_t = rolled(odd, 1), rolled(odd_t, 1)
-        after, after_t = rolled(even, -1), rolled(even_t, -1)
-        lo = low.reshape(1, CH)
-        one = [jnp.where(lo, before, even_t), jnp.where(lo, odd, after_t)]
-        two = [jnp.where(lo, before_t, even), jnp.where(lo, odd_t, after)]
-        both = [
-            jnp.concatenate(v, axis=1).reshape(count, pairs, 2 * CH) for v in (one, two)
+    def line_up(b):
+        parts = []
+        for g in range(groups):
+            x, y = [
+                pad[b, 2 * g + i].astype(f32).reshape(rows // 2, 8, CH) for i in range(2)
+            ]
+            turned_x, turned_y = pltpu.roll(x, 4, 1), pltpu.roll(y, 4, 1)
+            both = jnp.stack(
+                [jnp.where(upper, x, turned_y), jnp.where(upper, turned_x, y)], axis=1
+            )
+            parts.append(both.reshape(rows, 8, CH))
+        value = jnp.concatenate(parts, axis=1).reshape(rows * pairs, CH)
+        value = pltpu.roll(value, FIELDS, 1)
+        value = jnp.concatenate(
+            [
+                jnp.where(low, rolled(value, 1), value),
+                jnp.where(low, value, rolled(value, -1)),
+            ],
+            axis=1,
+        )
+        keep(quad, b, 0, value)
+
+    def keep(ref, b, at, value):
+        place = slice(at * pairs, at * pairs + value.shape[0])
+        ref[b, 0, place] = value.astype(bf16)
+        if at == 0:
+            ref[b, 1, : value.shape[0] - pairs] = value[pairs:].astype(bf16)
+        else:
+            ref[b, 1, place.start - pairs : place.stop - pairs] = value.astype(bf16)
+
+    def three(ref, b, at, count):
+        start, size = at * pairs, count * pairs
+        return [
+            ref[b, 0, start : start + size],
+            ref[b, 1, start : start + size],
+            ref[b, 0, start + 2 * pairs : start + 2 * pairs + size],
         ]
-        value = jnp.concatenate(both, axis=1).reshape(count * line, 2 * CH).astype(bf16)
-        quad[pl.ds(start * line, count * line), :] = value
-
-    step = 16
-    @pl.loop(0, rows // step)
-    def _(i):
-        line_up(pl.multiple_of(i * step, step), step)
+
+    def inside(value, at, count, depth, total, width):
+        above = max(0, min(depth, at + count) - at) * width
+        below = max(0, at + count - max(at, total - depth)) * width
+        parts = [value[:above] * top_scale] if above else []
+        parts.append(value[above : value.shape[0] - below])
+        if below:
+            parts.append(value[value.shape[0] - below :] * bottom_scale)
+        return jnp.concatenate(parts, axis=0)
 
     def dot(windows, weight):
         return silu(
@@ -134,77 +158,45 @@
     def window(ref, start, count, width, dy):
         return ref[pl.ds(pl.multiple_of((start + dy) * width, 8), count * width), :]
 
-    def clear(ref, depth, inner, width):
-        @pl.when(at_top)
-        def _():
-            ref[: depth * width] = jnp.zeros((depth * width, ref.shape[1]), ref.dtype)
-
-        @pl.when(at_bottom)
-        def _():
-            ref[(depth + inner) * width :] = jnp.zeros((depth * width, ref.shape[1]), ref.dtype)
-
-    def chunks(total, count, fn):
-        if total == count:
-            fn(0)
-        else:
-            @pl.loop(0, total // count)
-            def _(i):
-                fn(i * count)
-
-    count = h_first // FIRST_CHUNKS
-
-    def first_step(start):
-        v = dot([window(quad, start, count, line, dy) for dy in range(3)], c_in[...])
-        v = jnp.concatenate([v, sides(v)], axis=1).astype(bf16)
-        first[pl.ds(pl.multiple_of(start * line, 16), count * line), :] = v
-
-    chunks(h_first, count, first_step)
-    clear(first, 7, tile_rows, line)
-
-    count_s = h_skip // SKIP_CHUNKS
-
-    def skip_step(start):
-        v = dot([window(first, start, count_s, line, dy) for dy in range(3)], c_enc[...])
-        both = jnp.concatenate([v, sides(v)], axis=1).astype(bf16)
-        skip[pl.ds(start // 2, count_s // 2)] = both.reshape(count_s // 2, 2 * line, 4 * CH)
-        v = v.reshape(count_s // 2, 2 * line, 2 * CH)
-        v = (v[:, :line] + v[:, line:]).reshape(count_s // 2 * line, 2 * CH)
-        place = pl.ds(pl.multiple_of(start * line // 2, 8), count_s // 2 * line)
-        tmp[place, :] = (v[:, :CH] + v[:, CH:]) * 0.25
-
-    chunks(h_skip, count_s, skip_step)
-
-    @pl.when(at_top)
-    def _():
-        skip[:3] = jnp.zeros((3, 2 * line, 4 * CH), bf16)
-
-    @pl.when(at_bottom)
-    def _():
-        skip[h_pool - 3 :] = jnp.zeros((3, 2 * line, 4 * CH), bf16)
-
-    @pl.when(at_top)
-    def _():
-        tmp[: 3 * line] = jnp.zeros((3 * line, CH), f32)
-
-    @pl.when(at_bottom)
-    def _():
-        tmp[(h_pool - 3) * line :] = jnp.zeros((3 * line, CH), f32)
+    def encode(b):
+        line_up(b)
+        for at, count in split(h_first, FIRST_CHUNKS):
+            v = dot(three(quad, b, at, count), c_in[...])
+            v = inside(v, at, count, 7, h_first, pairs)
+            keep(first, b, at, jnp.concatenate([v, sides(v)], axis=1))
+        for at, count in split(h_skip, SKIP_CHUNKS):
+            v = dot(three(first, b, at, count), c_enc[...])
+            v = inside(v, at, count, 6, h_skip, pairs)
+            half_rows = count // 2
+            both = jnp.concatenate([v, sides(v)], axis=1).reshape(half_rows, 2, pairs, 4 * CH).astype(bf16)
+            for par in range(2):
+                place = par * line + b * pairs
+                skip[at // 2 : at // 2 + half_rows, place : place + pairs, :] = both[:, par]
+            v = v.reshape(half_rows, 2 * pairs, 2 * CH)
+            v = v[:, :pairs] + v[:, pairs:]
+            v = (v[:, :, :CH] + v[:, :, CH:]) * 0.25
+            for t in range(half_rows):
+                place = (at // 2 + t) * line + b * pairs
+                tmp[place : place + pairs, :] = v[t]
+
+    for b in range(2):
+        halo_here(b)
+        encode(b)
 
     size = h_pool * half
     v = jnp.concatenate([tmp[pl.ds(0, size, stride=2), :], tmp[pl.ds(1, size, stride=2), :]], axis=1)
     pooled[...] = jnp.concatenate([v, sides(v)], axis=1)
 
     v = dot([window(pooled, 0, h_mid, half, dy).astype(bf16) for dy in range(3)], c_m1[...])
+    v = inside(v, 0, h_mid, 2, h_mid, half)
     middle[...] = jnp.concatenate([v, sides(v)], axis=1)
-    clear(middle, 2, tile_rows // 2, half)
 
     v = dot([window(middle, 0, h_coarse, half, dy).astype(bf16) for dy in range(3)], c_m2[...])
     size = h_coarse * half
     tmp[pl.ds(0, size, stride=2), :] = v[:, :CH]
     tmp[pl.ds(1, size, stride=2), :] = v[:, CH:]
-    v = tmp[: 2 * size, :]
+    v = inside(tmp[: 2 * size, :], 0, h_coarse, 1, h_coarse, line)
     up[...] = jnp.concatenate([rolled(v, 1), v, rolled(v, -1)], axis=1).astype(bf16)
-    clear(up, 1, tile_rows // 2, line)
 
     def dec_step(par):
         def skip3(t, p):
@@ -216,6 +208,10 @@
             windows = [skip3(2, 1), skip3(3, 0), skip3(3, 1)]
         windows += [window(up, 0, h_dec, line, d) for d in range(2)]
         v = dot(windows, c_d1[par])
+        if par == 0:
+            v = jnp.concatenate([v[:line] * top_scale, v[line:]], axis=0)
+        else:
+            v = jnp.concatenate([v[:-line], v[-line:] * bottom_scale], axis=0)
 
         def compact(value):
             value = value.reshape(h_dec, 2, groups, 8, value.shape[1])
@@ -234,14 +230,6 @@
     dec_step(0)
     dec_step(1)
 
-    @pl.when(at_top)
-    def _():
-        dec[0] = jnp.zeros((2 * own, 4 * CH), bf16)
-
-    @pl.when(at_bottom)
-    def _():
-        dec[2 * h_dec - 1] = jnp.zeros((2 * own, 4 * CH), bf16)
-
 
 def tail_body(tile_rows, own, dec, c_d2, c_out, last, put):
     n = tile_rows // TAIL_CHUNKS
@@ -261,8 +249,7 @@
         put(i * n * own * 4, n * own * 4)
 
 
-TAIL_CHUNKS = 2
-FIRST_CHUNKS, SKIP_CHUNKS = 2, 2
+TAIL_CHUNKS = 1
 
 
 def unet_scratch(tile_rows, tile_cols):
@@ -270,8 +257,8 @@
     half = line // 2
     h_pool = (tile_rows + 12) // 2
     return [
-        pltpu.VMEM(((tile_rows + 2 * HALO) * line, 2 * CH), bf16),
-        pltpu.VMEM(((tile_rows + 14) * line, 4 * CH), bf16),
+        pltpu.VMEM((2, 2, (tile_rows + 2 * HALO) * half, 2 * CH), bf16),
+        pltpu.VMEM((2, 2, (tile_rows + 14) * half, 4 * CH), bf16),
         pltpu.VMEM((h_pool, 2 * line, 4 * CH), bf16),
         pltpu.VMEM((h_pool * line, CH), f32),
         pltpu.VMEM((h_pool * half, 4 * CH), f32),
@@ -303,11 +290,15 @@
             pltpu.make_async_copy(w_hbm[i], w_vmem[i], w_sem.at[i]).wait()
         prepare(*w_vmem, *mats, c_d2, c_out)
 
-    regrid_body(tile_rows, tile_cols, weights_start, weights_ready, *ins, pad, *own)
+    halo_here, sent = regrid_body(
+        tile_rows, tile_cols, weights_start, weights_ready, *ins, pad, *own
+    )
     row = lax.axis_index("row")
     unet_body(
-        tile_rows, tile_cols, row == 0, row == lax.axis_size("row") - 1, pad, mats, dec, *unet_refs
+        tile_rows, tile_cols, row == 0, row == lax.axis_size("row") - 1,
+        halo_here, pad, mats, dec, *unet_refs,
     )
+    sent()
 
 
 def tail_kernel(tile_rows, own, dec, c_d2, c_out, out_ref, last, staged, sem):
@@ -345,6 +336,9 @@
     )(dec, c_d2, c_out)
 
 
+EARLY = 0
+
+
 def regrid_body(
     tile_rows, tile_cols, weights_start, weights_ready, src_in, req_in, sten_in, wgt_in, pad,
     src_ref, req_ref, sten_ref, wgt_ref, load, asks, reqs, src_t, mix, outbox, inbox, acc, slot_rows, weight_rows,
@@ -401,8 +395,12 @@
     rows_beside = jnp.minimum(row, 1) + jnp.minimum(n_row - 1 - row, 1)
     pl.semaphore_wait(barrier, n - 1 + 3 * rows_beside)
 
+    def partner(step, sign):
+        chip = lax.rem(me // 2 + sign * (step // 2) + n, n // 2)
+        return chip * 2 + lax.rem(me + step, 2)
+
     def ask(step, sender):
-        dest = lax.rem(me + step, n)
+        dest = partner(step, 1)
         return pltpu.make_async_remote_copy(
             src_ref=asks.at[dest],
             dst_ref=reqs.at[sender],
@@ -413,8 +411,8 @@
         )
 
     @pl.loop(1, n)
-    def _(step):
-        ask(step, me).start()
+    def _(i):
+        ask(n - i, me).start()
 
     reqs[me] = asks[me]
     loads[1].wait()
@@ -468,7 +466,7 @@
                         total = part if total is None else total + part
                     mix[j, start + g : start + g + tile, here] = total
 
-    @pl.loop(0, n // 2)
+    @pl.loop(0, EARLY)
     def _(j):
         mix_block(j)
 
@@ -485,51 +483,57 @@
         hot = jnp.concatenate(rows, axis=0)
         return jnp.dot(src_t[...], hot, preferred_element_type=f32).astype(bf16)
 
-    def post(step, sender):
+    def post(step, sender, b):
+        part = slice(b * FIELDS, (b + 1) * FIELDS)
         return pltpu.make_async_remote_copy(
-            src_ref=outbox.at[step],
-            dst_ref=inbox.at[sender],
-            send_sem=box_send.at[step],
-            recv_sem=box_recv.at[sender],
-            device_id=(row, lax.rem(me + step, n)),
+            src_ref=outbox.at[step, part],
+            dst_ref=inbox.at[sender, part],
+            send_sem=box_send.at[b, step],
+            recv_sem=box_recv.at[b, sender],
+            device_id=(row, partner(step, 1)),
             device_id_type=MESH,
         )
 
     @pl.loop(1, n)
-    def _(step):
-        dest = lax.rem(me + step, n)
+    def _(i):
+        step = n - i
+        dest = partner(step, 1)
         ask(step, dest).wait_recv()
         outbox[step] = picked(dest)
-        post(step, me).start()
+        post(step, me, 0).start()
+
+    @pl.loop(1, n)
+    def _(i):
+        post(n - i, me, 1).start()
 
     inbox[me] = picked(me)
 
-    @pl.loop(n // 2, n)
+    @pl.loop(EARLY, n)
     def _(j):
         mix_block(j)
 
-    acc[...] = jnp.dot(inbox[me], mix[me], preferred_element_type=f32)
-    weights_ready()
-
-    @pl.loop(1, n)
-    def _(step):
-        sender = lax.rem(me - step + n, n)
-        post(step, sender).wait_recv()
-        acc[...] += jnp.dot(inbox[sender], mix[sender], preferred_element_type=f32)
-
-    for par in range(2):
-        turned = acc[:, par * spots // 2 : (par + 1) * spots // 2].T.astype(bf16)
-        lanes_here = slice(par * CH, (par + 1) * CH)
+    def gather(b):
+        part = slice(b * FIELDS, (b + 1) * FIELDS)
+        acc[...] = jnp.dot(inbox[me, part], mix[me], preferred_element_type=f32)
+
+        @pl.loop(1, n)
+        def _(i):
+            step = n - i
+            sender = partner(step, -1)
+            post(step, sender, b).wait_recv()
+            acc[...] += jnp.dot(inbox[sender, part], mix[sender], preferred_element_type=f32)
+
+        turned = jnp.concatenate([acc[:, : spots // 2], acc[:, spots // 2 :]], axis=0).T.astype(bf16)
         for xb in range(blocks):
-            pad[xb + 1, edge : edge + inner, lanes_here] = turned[xb * inner : (xb + 1) * inner]
-
-    @pl.when(jnp.logical_not(has_up))
-    def _():
-        pad[:, :edge] = jnp.zeros((blocks + 2, edge, 2 * CH), bf16)
-
-    @pl.when(jnp.logical_not(has_down))
-    def _():
-        pad[:, edge + inner :] = jnp.zeros((blocks + 2, edge, 2 * CH), bf16)
+            pad[b, xb + 1, edge : edge + inner] = turned[xb * inner : (xb + 1) * inner]
+
+        @pl.when(jnp.logical_not(has_up))
+        def _():
+            pad[b, :, :edge] = jnp.zeros((blocks + 2, edge, CH), bf16)
+
+        @pl.when(jnp.logical_not(has_down))
+        def _():
+            pad[b, :, edge + inner :] = jnp.zeros((blocks + 2, edge, CH), bf16)
 
     mid = slice(edge, edge + inner)
     first, last = slice(edge, 2 * edge), slice(inner, inner + edge)
@@ -548,57 +552,74 @@
         (-1, -1, (left, first), (after, high)),
     ]
 
-    def shift(i):
+    def shift(i, b):
         dr, dc, src, dst = moves[i]
         return pltpu.make_async_remote_copy(
-            src_ref=pad.at[src[0], src[1]],
-            dst_ref=pad.at[dst[0], dst[1]],
-            send_sem=halo_send.at[i],
-            recv_sem=halo_recv.at[i],
+            src_ref=pad.at[b, src[0], src[1]],
+            dst_ref=pad.at[b, dst[0], dst[1]],
+            send_sem=halo_send.at[b, i],
+            recv_sem=halo_recv.at[b, i],
             device_id=(row + dr, lax.rem(me + dc + n, n)),
             device_id_type=MESH,
         )
 
-    @pl.when(has_down)
-    def _():
-        for i in (2, 3, 4):
-            shift(i).start()
-
-    @pl.when(has_up)
-    def _():
-        for i in (5, 6, 7):
-            shift(i).start()
-
-    for i in (0, 1):
-        shift(i).start()
-
-    @pl.loop(1, n)
-    def _(step):
-        ask(step, me).wait_send()
-        post(step, me).wait_send()
-
-    for i in (0, 1):
-        shift(i).wait()
-
-    @pl.when(has_up)
-    def _():
-        for i in (2, 3, 4):
-            shift(i).wait_recv()
-
-    @pl.when(has_down)
-    def _():
-        for i in (5, 6, 7):
-            shift(i).wait_recv()
-
-    @pl.when(has_down)
-    def _():
-        for i in (2, 3, 4):
-            shift(i).wait_send()
-
-    @pl.when(has_up)
-    def _():
-        for i in (5, 6, 7):
-            shift(i).wait_send()
+    def halo_start(b):
+        @pl.when(has_down)
+        def _():
+            for i in (2, 3, 4):
+                shift(i, b).start()
+
+        @pl.when(has_up)
+        def _():
+            for i in (5, 6, 7):
+                shift(i, b).start()
+
+        for i in (0, 1):
+            shift(i, b).start()
+
+    def halo_here(b):
+        for i in (0, 1):
+            shift(i, b).wait_recv()
+
+        @pl.when(has_up)
+        def _():
+            for i in (2, 3, 4):
+                shift(i, b).wait_recv()
+
+        @pl.when(has_down)
+        def _():
+            for i in (5, 6, 7):
+                shift(i, b).wait_recv()
+
+    def sent():
+        @pl.loop(1, n)
+        def _(step):
+            ask(step, me).wait_send()
+            for b in range(2):
+                post(step, me, b).wait_send()
+
+        for b in range(2):
+            for i in (0, 1):
+                shift(i, b).wait_send()
+
+        @pl.when(has_down)
+        def _():
+            for b in range(2):
+                for i in (2, 3, 4):
+                    shift(i, b).wait_send()
+
+        @pl.when(has_up)
+        def _():
+            for b in range(2):
+                for i in (5, 6, 7):
+                    shift(i, b).wait_send()
+
+    gather(0)
+    halo_start(0)
+    weights_ready()
+    gather(1)
+    halo_start(1)
+    return halo_here, sent
 
 
 def forward(source, wanted, stencil, weight, weights, tile_rows, tile_cols):
@@ -621,7 +642,7 @@
         + [dma((7,))]
         + weight_scratch()
         + [
-            pltpu.VMEM((blocks + 2, rows * HALO // 2, 2 * columns), bf16),
+            pltpu.VMEM((2, blocks + 2, rows * HALO // 2, columns), bf16),
             pltpu.VMEM(source.shape, bf16),
             pltpu.VMEM(wanted.shape, jnp.int32),
             pltpu.VMEM(stencil.shape, jnp.int32),
@@ -633,10 +654,10 @@
             pltpu.VMEM((n, cap, spots), bf16),
             pltpu.VMEM((n, columns, cap), bf16),
             pltpu.VMEM((n, columns, cap), bf16),
-            pltpu.VMEM((columns, spots), f32),
+            pltpu.VMEM((FIELDS, spots), f32),
             pltpu.VMEM((taps, spots), f32),
             pltpu.VMEM((taps, spots), f32),
-            dma((n,)), dma((n,)), dma((n,)), dma((n,)), dma((8,)), dma((8,)),
+            dma((n,)), dma((n,)), dma((2, n)), dma((2, n)), dma((2, 8)), dma((2, 8)),
         ]
         + unet_scratch(tile_rows, tile_cols),
         compiler_params=pltpu.CompilerParams(

time: 32.2 us -> 28.7 us (0.89)
  Pallas kernels: 32 us -> 28.5 us
    pallas_call x1, Pallas kernels: 29.2 us -> 26.4 us  [forward(): pl.pallas_call(functools.partial(whole_kernel, tile_rows, tile_cols), out...]
    pallas_call x1, Pallas kernels: 2.8 us -> 2.11 us  [tail(): pl.pallas_call(functools.partial(tail_kernel, tile_rows, tile_cols // 2),...]
where the time goes in v4:
time: 28.7 us; the launch traced here: 28.5 us
  Pallas kernels  28.5 us (99%)
    pallas_call x1, Pallas kernels, forward(): pl.pallas_call(functools.partial(whole_kernel, tile_rows, tile_cols), out...  26.4 us
    pallas_call x1, Pallas kernels, tail(): pl.pallas_call(functools.partial(tail_kernel, tile_rows, tile_cols // 2),...  2.11 us

profile of v4, /device:TPU:0, one launch (start us, length us, event | category | flops | bytes accessed | tf_op | source)
XLA Modules:
  0.0 28.5 jit_solution(975761061526478470)
XLA Ops:
  0.0 26.4 %shard_map.109 = (bf16[34,32,512]{2,1,0:T(8,128)(2,1)S(1)}, bf16[1536,256]{1,0:T(8,128)(2,1)S(1)}, bf16[256,256]{1,0:T(8,128)(2,1)S(1)}) custom-call(bf16[1024,128]{1,0:T(8,128)(2,1)} %bitcast.10, s32[8,256]{1,0:T(8,128)} %bitcast.14, s32[128,32]{1,0:T(8,128)} %bitcast.11, f32[128,32]{1,0:T(8,128)} %bitcast.12, bf16[3,3,64,128]{3,2,1,0:T(8,128)(2,1)} %refs_4_.1, ...), custom_call_target="tpu_custom_call" | custom-call | flops 1000000000 | bytes 2000000 | tf_op jit(solution)/shard_map/pallas_call | solution.py:633
  26.4 2.1 %shard_map.110 = bf16[2048,64]{1,0:T(8,128)(2,1)} custom-call(bf16[34,32,512]{2,1,0:T(8,128)(2,1)S(1)} %get-tuple-element.8.dec, bf16[1536,256]{1,0:T(8,128)(2,1)S(1)} %get-tuple-element.9.c_d2, bf16[256,256]{1,0:T(8,128)(2,1)S(1)} %get-tuple-element.10.c_out), custom_call_target="tpu_custom_call" | custom-call | flops 1000000000 | bytes 2000000 | tf_op jit(solution)/shard_map/pallas_call | solution.py:322

commit v5 on v4

--- a/solution.py
+++ b/solution.py
@@ -80,7 +80,7 @@
     return tile_cols // 2 + HALO
 
 
-def unet_body(tile_rows, tile_cols, at_top, at_bottom, halo_here, pad, weights, dec, quad, first, skip, tmp, pooled, middle, up):
+def unet_body(tile_rows, tile_cols, at_top, at_bottom, halo_here, pad, weights, dec, quad, first, skip, tmp, pooled, middle, up, part):
     c_in, c_enc, c_m1, c_m2, c_d1 = weights
     rows = tile_rows + 2 * HALO
     pairs = pairs_of(tile_cols)
@@ -168,16 +168,30 @@
             v = dot(three(first, b, at, count), c_enc[...])
             v = inside(v, at, count, 6, h_skip, pairs)
             half_rows = count // 2
-            both = jnp.concatenate([v, sides(v)], axis=1).reshape(half_rows, 2, pairs, 4 * CH).astype(bf16)
+            both = jnp.concatenate([v, sides(v)], axis=1).reshape(half_rows, 2, pairs, 4 * CH)
             for par in range(2):
-                place = par * line + b * pairs
-                skip[at // 2 : at // 2 + half_rows, place : place + pairs, :] = both[:, par]
+                piece = both[:, par].reshape(half_rows * pairs, 4 * CH)
+                place = at // 2 * pairs
+                skip[b, 0, par, place : place + half_rows * pairs] = piece.astype(bf16)
+                if at == 0:
+                    piece = piece[pairs:]
+                else:
+                    place -= pairs
+                skip[b, 1, par, place : place + piece.shape[0]] = piece.astype(bf16)
             v = v.reshape(half_rows, 2 * pairs, 2 * CH)
             v = v[:, :pairs] + v[:, pairs:]
             v = (v[:, :, :CH] + v[:, :, CH:]) * 0.25
             for t in range(half_rows):
                 place = (at // 2 + t) * line + b * pairs
                 tmp[place : place + pairs, :] = v[t]
+        for par in range(2):
+            size = h_dec * pairs
+            windows = [
+                skip[b, d // 2, d % 2, 2 * pairs : 2 * pairs + size] for d in range(par, par + 3)
+            ]
+            part[b, par] = jnp.dot(
+                jnp.concatenate(windows, axis=1), c_d1[par, : 12 * CH], preferred_element_type=f32
+            )
 
     for b in range(2):
         halo_here(b)
@@ -196,39 +210,28 @@
     tmp[pl.ds(0, size, stride=2), :] = v[:, :CH]
     tmp[pl.ds(1, size, stride=2), :] = v[:, CH:]
     v = inside(tmp[: 2 * size, :], 0, h_coarse, 1, h_coarse, line)
-    up[...] = jnp.concatenate([rolled(v, 1), v, rolled(v, -1)], axis=1).astype(bf16)
-
-    def dec_step(par):
-        def skip3(t, p):
-            return skip[t : t + h_dec, p * line : (p + 1) * line, :].reshape(h_dec * line, 4 * CH)
-
-        if par == 0:
-            windows = [skip3(2, 0), skip3(2, 1), skip3(3, 0)]
-        else:
-            windows = [skip3(2, 1), skip3(3, 0), skip3(3, 1)]
-        windows += [window(up, 0, h_dec, line, d) for d in range(2)]
-        v = dot(windows, c_d1[par])
-        if par == 0:
-            v = jnp.concatenate([v[:line] * top_scale, v[line:]], axis=0)
-        else:
-            v = jnp.concatenate([v[:-line], v[-line:] * bottom_scale], axis=0)
-
-        def compact(value):
-            value = value.reshape(h_dec, 2, groups, 8, value.shape[1])
-            turned = [pltpu.roll(value[:, :, g].reshape(h_dec * 2, 8, -1), 4, 1) for g in range(groups)]
-            parts = [
-                jnp.where(upper, turned[g], turned[g + 1]).reshape(h_dec, 2, 8, -1)
-                for g in range(groups - 1)
-            ]
-            return jnp.concatenate(parts, axis=2).reshape(h_dec, 2 * own, -1)
-
-        both = jnp.concatenate([compact(v), compact(sides(v))], axis=2)
-        both = both.astype(bf16)
-        for i in range(h_dec):
-            dec[2 * i + par] = both[i]
-
-    dec_step(0)
-    dec_step(1)
+    v = jnp.concatenate([rolled(v, 1), v, rolled(v, -1)], axis=1).reshape(h_coarse, line, 3 * CH)
+    for b in range(2):
+        piece = v[:, b * pairs : (b + 1) * pairs].reshape(h_coarse * pairs, 3 * CH)
+        up[b] = jnp.concatenate([piece[:-pairs], piece[pairs:]], axis=1).astype(bf16)
+
+    def compact(value):
+        value = value.reshape(h_dec, groups, 8, value.shape[1])
+        turned = [pltpu.roll(value[:, g], 4, 1) for g in range(groups)]
+        parts = [jnp.where(upper, turned[g], turned[g + 1]) for g in range(groups - 1)]
+        return jnp.concatenate(parts, axis=1)
+
+    for b in range(2):
+        for par in range(2):
+            v = part[b, par] + jnp.dot(up[b], c_d1[par, 12 * CH :], preferred_element_type=f32)
+            v = silu(v)
+            if par == 0:
+                v = jnp.concatenate([v[:pairs] * top_scale, v[pairs:]], axis=0)
+            else:
+                v = jnp.concatenate([v[:-pairs], v[-pairs:] * bottom_scale], axis=0)
+            both = jnp.concatenate([compact(v), compact(sides(v))], axis=2).astype(bf16)
+            for i in range(h_dec):
+                dec[2 * i + par, b * own : (b + 1) * own] = both[i]
 
 
 def tail_body(tile_rows, own, dec, c_d2, c_out, last, put):
@@ -259,11 +262,12 @@
     return [
         pltpu.VMEM((2, 2, (tile_rows + 2 * HALO) * half, 2 * CH), bf16),
         pltpu.VMEM((2, 2, (tile_rows + 14) * half, 4 * CH), bf16),
-        pltpu.VMEM((h_pool, 2 * line, 4 * CH), bf16),
+        pltpu.VMEM((2, 2, 2, h_pool * half, 4 * CH), bf16),
         pltpu.VMEM((h_pool * line, CH), f32),
         pltpu.VMEM((h_pool * half, 4 * CH), f32),
         pltpu.VMEM(((h_pool - 2) * half, 4 * CH), f32),
-        pltpu.VMEM(((h_pool - 4) * line, 3 * CH), bf16),
+        pltpu.VMEM((2, (h_pool - 5) * half, 6 * CH), bf16),
+        pltpu.VMEM((2, 2, (h_pool - 5) * half, 2 * CH), f32),
     ]
 
 
@@ -514,14 +518,23 @@
 
     def gather(b):
         part = slice(b * FIELDS, (b + 1) * FIELDS)
-        acc[...] = jnp.dot(inbox[me, part], mix[me], preferred_element_type=f32)
-
-        @pl.loop(1, n)
+        post(1, partner(1, -1), b).wait_recv()
+        total = jnp.dot(inbox[me, part], mix[me], preferred_element_type=f32)
+        beside = partner(1, -1)
+        acc[...] = total + jnp.dot(inbox[beside, part], mix[beside], preferred_element_type=f32)
+
+        @pl.loop(1, n // 2)
         def _(i):
-            step = n - i
-            sender = partner(step, -1)
-            post(step, sender, b).wait_recv()
-            acc[...] += jnp.dot(inbox[sender, part], mix[sender], preferred_element_type=f32)
+            senders = []
+            for step in (n - 2 * i + 1, n - 2 * i):
+                sender = partner(step, -1)
+                post(step, sender, b).wait_recv()
+                senders.append(sender)
+            left, right = [
+                jnp.dot(inbox[sender, part], mix[sender], preferred_element_type=f32)
+                for sender in senders
+            ]
+            acc[...] += left + right
 
         turned = jnp.concatenate([acc[:, : spots // 2], acc[:, spots // 2 :]], axis=0).T.astype(bf16)
         for xb in range(blocks):

time: 28.7 us -> 28 us (0.976)
  Pallas kernels: 28.5 us -> 27.8 us
    pallas_call x1, Pallas kernels: 26.4 us -> 25.7 us  [forward(): pl.pallas_call(functools.partial(whole_kernel, tile_rows, tile_cols), out...]
where the time goes in v5:
time: 28 us; the launch traced here: 27.8 us
  Pallas kernels  27.8 us (99%)
    pallas_call x1, Pallas kernels, forward(): pl.pallas_call(functools.partial(whole_kernel, tile_rows, tile_cols), out...  25.7 us
    pallas_call x1, Pallas kernels, tail(): pl.pallas_call(functools.partial(tail_kernel, tile_rows, tile_cols // 2),...  2.11 us

profile of v5, /device:TPU:0, one launch (start us, length us, event | category | flops | bytes accessed | tf_op | source)
XLA Modules:
  0.0 27.8 jit_solution(4267074915290865581)
XLA Ops:
  0.0 25.7 %shard_map.109 = (bf16[34,32,512]{2,1,0:T(8,128)(2,1)S(1)}, bf16[1536,256]{1,0:T(8,128)(2,1)S(1)}, bf16[256,256]{1,0:T(8,128)(2,1)S(1)}) custom-call(bf16[1024,128]{1,0:T(8,128)(2,1)} %bitcast.10, s32[8,256]{1,0:T(8,128)} %bitcast.14, s32[128,32]{1,0:T(8,128)} %bitcast.11, f32[128,32]{1,0:T(8,128)} %bitcast.12, bf16[3,3,64,128]{3,2,1,0:T(8,128)(2,1)} %refs_4_.1, ...), custom_call_target="tpu_custom_call" | custom-call | flops 1000000000 | bytes 2000000 | tf_op jit(solution)/shard_map/pallas_call | solution.py:646
  25.7 2.1 %shard_map.110 = bf16[2048,64]{1,0:T(8,128)(2,1)} custom-call(bf16[34,32,512]{2,1,0:T(8,128)(2,1)S(1)} %get-tuple-element.8.dec, bf16[1536,256]{1,0:T(8,128)(2,1)S(1)} %get-tuple-element.9.c_d2, bf16[256,256]{1,0:T(8,128)(2,1)S(1)} %get-tuple-element.10.c_out), custom_call_target="tpu_custom_call" | custom-call | flops 1000000000 | bytes 2000000 | tf_op jit(solution)/shard_map/pallas_call | solution.py:326

commit v6 on v5

--- a/solution.py
+++ b/solution.py
@@ -15,14 +15,17 @@
 
 
 def silu(a):
-    return a * (0.5 + 0.5 * jnp.tanh(0.5 * a))
+    return a + a * jnp.tanh(a)
+
+
+def halved(w):
+    return (w.astype(f32) * 0.5).astype(bf16)
 
 
 def pair_weight(out, base, w, dy):
     zero = jnp.zeros((CH, CH), bf16)
-    rows = [
-        (w[dy, 1], w[dy, 0]), (w[dy, 2], w[dy, 1]), (w[dy, 0], zero), (zero, w[dy, 2])
-    ]
+    left, middle, right = [halved(w[dy, dx]) for dx in range(3)]
+    rows = [(middle, left), (right, middle), (left, zero), (zero, right)]
     for i, (even, odd) in enumerate(rows):
         place = slice(base + i * CH, base + (i + 1) * CH)
         out[place, :CH] = even
@@ -35,8 +38,8 @@
     for dy in range(3):
         for j in range(4):
             place = slice(dy * quad + j * FIELDS, dy * quad + (j + 1) * FIELDS)
-            c_in[place, :CH] = w_in[dy, j] if j < 3 else none
-            c_in[place, CH:] = w_in[dy, j - 1] if j > 0 else none
+            c_in[place, :CH] = halved(w_in[dy, j]) if j < 3 else none
+            c_in[place, CH:] = halved(w_in[dy, j - 1]) if j > 0 else none
         base = dy * 4 * CH
         pair_weight(c_enc, base, w_enc, dy)
         pair_weight(c_m1, base, w_m1, dy)
@@ -48,7 +51,7 @@
     for par in range(2):
         groups = ((0, 1), (2,)) if par == 0 else ((0,), (1, 2))
         for g, dys in enumerate(groups):
-            taps = [sum(w_d1[dy, dx, :CH].astype(f32) for dy in dys) for dx in range(3)]
+            taps = [0.5 * sum(w_d1[dy, dx, :CH].astype(f32) for dy in dys) for dx in range(3)]
             base = 12 * CH + g * 3 * CH
             rows = [
                 (taps[0].astype(bf16), zero),
@@ -280,10 +283,10 @@
 
 
 def whole_kernel(tile_rows, tile_cols, *refs):
-    ins, w_hbm, outs, scratch = refs[:4], refs[4:11], refs[11:14], refs[14:]
+    ins, w_hbm, out_ref, scratch = refs[:4], refs[4:11], refs[11], refs[12:]
     w_vmem, w_sem, mats = scratch[:7], scratch[7], scratch[8:13]
-    pad, own, unet_refs = scratch[13], scratch[14:34], scratch[34:]
-    dec, c_d2, c_out = outs
+    pad, own, unet_refs = scratch[13], scratch[14:34], scratch[34:-4]
+    dec, c_d2, c_out, last = scratch[-4:]
 
     def weights_start():
         for i in range(7):
@@ -302,42 +305,29 @@
         tile_rows, tile_cols, row == 0, row == lax.axis_size("row") - 1,
         halo_here, pad, mats, dec, *unet_refs,
     )
-    sent()
-
-
-def tail_kernel(tile_rows, own, dec, c_d2, c_out, out_ref, last, staged, sem):
-    copies = []
 
     def put(start, count):
         place = slice(start, start + count)
-        staged[place, :] = last[place, :FIELDS].astype(bf16)
-        copy = pltpu.make_async_copy(staged.at[place], out_ref.at[place], sem.at[len(copies)])
-        copy.start()
-        copies.append(copy)
-
-    tail_body(tile_rows, own, dec, c_d2, c_out, last, put)
-    for copy in copies:
-        copy.wait()
-
-
-def tail(dec, c_d2, c_out):
-    tile_rows, tile_cols = dec.shape[0] - 2, dec.shape[1]
-    cells = 2 * tile_rows * tile_cols
+        out_ref[place, :] = last[place, :FIELDS].astype(bf16)
+
+    tail_body(tile_rows, tile_cols // 2, dec, c_d2, c_out, last, put)
+    sent()
+
+
+def write_kernel(value, out_ref, sem):
+    copy = pltpu.make_async_copy(value, out_ref, sem)
+    copy.start()
+    copy.wait()
+
+
+def write(value):
     return pl.pallas_call(
-        functools.partial(tail_kernel, tile_rows, tile_cols // 2),
-        out_shape=jax.ShapeDtypeStruct((cells, FIELDS), bf16),
-        in_specs=[pl.BlockSpec(memory_space=pltpu.VMEM)] * 3,
+        write_kernel,
+        out_shape=jax.ShapeDtypeStruct(value.shape, bf16),
+        in_specs=[pl.BlockSpec(memory_space=pltpu.VMEM)],
         out_specs=pl.BlockSpec(memory_space=pltpu.HBM),
-        scratch_shapes=[
-            pltpu.VMEM((cells, CH), f32),
-            pltpu.VMEM((cells, FIELDS), bf16),
-            pltpu.SemaphoreType.DMA((TAIL_CHUNKS,)),
-        ],
-        compiler_params=pltpu.CompilerParams(vmem_limit_bytes=16 * 1024 * 1024),
-        cost_estimate=pl.CostEstimate(
-            flops=10**9, bytes_accessed=2 * 10**6, transcendentals=0
-        ),
-    )(dec, c_d2, c_out)
+        scratch_shapes=[pltpu.SemaphoreType.DMA],
+    )(pltpu.with_memory_space_constraint(value, pltpu.VMEM))
 
 
 EARLY = 0
@@ -645,12 +635,9 @@
     dma = pltpu.SemaphoreType.DMA
     return pl.pallas_call(
         functools.partial(whole_kernel, tile_rows, tile_cols),
-        out_shape=[
-            pltpu.VMEM(shape, bf16)
-            for shape in ((tile_rows + 2, tile_cols, 4 * CH), (12 * CH, 2 * CH), (2 * CH, 2 * CH))
-        ],
+        out_shape=pltpu.VMEM((2 * spots, FIELDS), bf16),
         in_specs=[pl.BlockSpec(memory_space=pltpu.HBM)] * 11,
-        out_specs=[pl.BlockSpec(memory_space=pltpu.VMEM)] * 3,
+        out_specs=pl.BlockSpec(memory_space=pltpu.VMEM),
         scratch_shapes=[pltpu.VMEM(w.shape, bf16) for w in weights]
         + [dma((7,))]
         + weight_scratch()
@@ -672,7 +659,13 @@
             pltpu.VMEM((taps, spots), f32),
             dma((n,)), dma((n,)), dma((2, n)), dma((2, n)), dma((2, 8)), dma((2, 8)),
         ]
-        + unet_scratch(tile_rows, tile_cols),
+        + unet_scratch(tile_rows, tile_cols)
+        + [
+            pltpu.VMEM((tile_rows + 2, tile_cols, 4 * CH), bf16),
+            pltpu.VMEM((12 * CH, 2 * CH), bf16),
+            pltpu.VMEM((2 * CH, 2 * CH), bf16),
+            pltpu.VMEM((2 * spots, CH), f32),
+        ],
         compiler_params=pltpu.CompilerParams(
             collective_id=0, has_side_effects=True, vmem_limit_bytes=40 * 1024 * 1024
         ),
@@ -694,7 +687,7 @@
         tile_rows,
         tile_cols,
     )
-    return tail(*done).reshape(tile_rows, tile_cols, 2, FIELDS)
+    return write(done).reshape(tile_rows, tile_cols, 2, FIELDS)
 
 
 def solution(mesh):

time: 28 us -> 27.6 us (0.986)
  Pallas kernels: 27.8 us -> 27.4 us
    pallas_call x1, Pallas kernels: 2.11 us -> 0.8 us  [write(): pl.pallas_call(write_kernel, out_shape=jax.ShapeDtypeStruct(value.shape,...]
    pallas_call x1, Pallas kernels: 25.7 us -> 26.6 us  [forward(): pl.pallas_call(functools.partial(whole_kernel, tile_rows, tile_cols), out...]
where the time goes in v6:
time: 27.6 us; the launch traced here: 27.4 us
  Pallas kernels  27.4 us (99%)
    pallas_call x1, Pallas kernels, forward(): pl.pallas_call(functools.partial(whole_kernel, tile_rows, tile_cols), out...  26.6 us
    pallas_call x1, Pallas kernels, write(): pl.pallas_call(write_kernel, out_shape=jax.ShapeDtypeStruct(value.shape,...  0.8 us

profile of v6, /device:TPU:0, one launch (start us, length us, event | category | flops | bytes accessed | tf_op | source)
XLA Modules:
  0.0 27.4 jit_solution(12224315763237666114)
XLA Ops:
  0.0 26.6 %shard_map.109.value = bf16[2048,64]{1,0:T(8,128)(2,1)S(1)} custom-call(bf16[1024,128]{1,0:T(8,128)(2,1)} %bitcast.10, s32[8,256]{1,0:T(8,128)} %bitcast.14, s32[128,32]{1,0:T(8,128)} %bitcast.11, f32[128,32]{1,0:T(8,128)} %bitcast.12, bf16[3,3,64,128]{3,2,1,0:T(8,128)(2,1)} %refs_4_.1, bf16[3,3,128,128]{3,2,1,0:T(8,128)(2,1)} %refs_5_.1, ...), custom_call_target="tpu_custom_call" | custom-call | flops 1000000000 | bytes 2000000 | tf_op jit(solution)/shard_map/pallas_call | solution.py:636
  26.6 0.8 %shard_map.110 = bf16[2048,64]{1,0:T(8,128)(2,1)} custom-call(bf16[2048,64]{1,0:T(8,128)(2,1)S(1)} %shard_map.109.value), custom_call_target="tpu_custom_call" | custom-call | tf_op jit(solution)/shard_map/pallas_call | solution.py:324

commit v7 on v6

--- a/solution.py
+++ b/solution.py
@@ -76,7 +76,7 @@
     return [(at, min(size, total - at)) for at in range(0, total, size)]
 
 
-FIRST_CHUNKS, SKIP_CHUNKS = 2, 2
+FIRST_CHUNKS, SKIP_CHUNKS = 3, 2
 
 
 def pairs_of(tile_cols):

time: 27.6 us -> 27.5 us (level)
  no operation moved by 1% of the time
where the time goes in v7:
time: 27.5 us; the launch traced here: 27.3 us
  Pallas kernels  27.3 us (99%)
    pallas_call x1, Pallas kernels, forward(): pl.pallas_call(functools.partial(whole_kernel, tile_rows, tile_cols), out...  26.5 us
    pallas_call x1, Pallas kernels, write(): pl.pallas_call(write_kernel, out_shape=jax.ShapeDtypeStruct(value.shape,...  0.8 us

profile of v7, /device:TPU:0, one launch (start us, length us, event | category | flops | bytes accessed | tf_op | source)
XLA Modules:
  0.0 27.3 jit_solution(1286825901903887861)
XLA Ops:
  0.0 26.5 %shard_map.109.value = bf16[2048,64]{1,0:T(8,128)(2,1)S(1)} custom-call(bf16[1024,128]{1,0:T(8,128)(2,1)} %bitcast.10, s32[8,256]{1,0:T(8,128)} %bitcast.14, s32[128,32]{1,0:T(8,128)} %bitcast.11, f32[128,32]{1,0:T(8,128)} %bitcast.12, bf16[3,3,64,128]{3,2,1,0:T(8,128)(2,1)} %refs_4_.1, bf16[3,3,128,128]{3,2,1,0:T(8,128)(2,1)} %refs_5_.1, ...), custom_call_target="tpu_custom_call" | custom-call | flops 1000000000 | bytes 2000000 | tf_op jit(solution)/shard_map/pallas_call | solution.py:636
  26.5 0.8 %shard_map.110 = bf16[2048,64]{1,0:T(8,128)(2,1)} custom-call(bf16[2048,64]{1,0:T(8,128)(2,1)S(1)} %shard_map.109.value), custom_call_target="tpu_custom_call" | custom-call | tf_op jit(solution)/shard_map/pallas_call | solution.py:324
